TPU v7x, 32 devices: a whole 2x2x4 slice. The times are simulated.
32 devices in a mesh: rows: 8 (over y, x, core), kc: 4 (over z).
Axes of the slice: x: 2, y: 2, z: 4, core: 2. Of those that a mesh axis runs over, the one named last changes fastest.
Arguments:
- inputs: bfloat16 [4, 2048, 768], P(None, ('rows', 'kc')), may hold values from -6 to 6
- w_query: bfloat16 [768, 768], replicated, may hold values from -0.4375 to 0.4375
- w_key: bfloat16 [768, 768], replicated, may hold values from -0.21875 to 0.21875
- w_value: bfloat16 [768, 768], replicated, may hold values from -0.21875 to 0.21875
- w_out: bfloat16 [768, 768], replicated, may hold values from -1.25 to 1.25
- w_up: bfloat16 [768, 3072], replicated, may hold values from -0.21875 to 0.21875
- w_down: bfloat16 [3072, 768], replicated, may hold values from -0.109375 to 0.109375
- gain_attn: float32 [768], replicated, may hold values from 0.5 to 1.5
- gain_ffn: float32 [768], replicated, may hold values from 0.5 to 1.5
- proj_e: bfloat16 [256, 256], P(None, 'kc'), may hold values from -0.375 to 0.375
- lengths: int32 [4, 8], P(None, 'rows'), may hold values from 16 to 256, as said below
- cotangent: bfloat16 [4, 2048, 768], P(None, ('rows', 'kc')), may hold values from -6 to 6
Outputs:
- output: bfloat16 [4, 2048, 768], P(None, ('rows', 'kc'))
- grad_inputs: bfloat16 [4, 2048, 768], P(None, ('rows', 'kc'))
- grad_query: float32 [768, 768], P('rows', 'kc')
- grad_key: float32 [768, 768], P('rows', 'kc')
- grad_value: float32 [768, 768], P('rows', 'kc')
- grad_out: float32 [768, 768], P('rows', 'kc')
- grad_up: float32 [768, 3072], P('rows', 'kc')
- grad_down: float32 [3072, 768], P('rows', 'kc')
- grad_gain_attn: float32 [768], P('rows')
- grad_gain_ffn: float32 [768], P('rows')
- grad_proj_e: float32 [256, 256], P('rows', 'kc')
Inputs may be any that keep to these rules, and one draw needn't show every extreme that they name: `lengths`: for every sequence index g, one micro-batch holds a sequence of the full 256 positions.
All inputs are finite; a program needn't handle non-finite values.
Results may differ from a plain program's by a relative error of at most 0.018.
Values may be sent and summed in bfloat16 or wider, within the bound.
No kernel may reach another device: no remote copies, remote signals or barrier semaphores. Data moves between devices by JAX's collectives and lax.ppermute only.
A program may use at most 192 MiB of HBM per device.

v0:
```python
import jax
import jax.numpy as jnp
from jax import lax
from jax.sharding import PartitionSpec as P

HEAD = 64


def normed(values, norm_gain):
    row_mean = jnp.mean(values, axis=-1, keepdims=True)
    centred = values - row_mean
    return (
        centred * lax.rsqrt(jnp.mean(centred * centred, axis=-1, keepdims=True) + 1e-05) * norm_gain
    )


def times_plain(left, right):
    return jnp.dot(left, right, preferred_element_type=jnp.float32)


def times_trans(left, right):
    return jnp.einsum("ta,ba->tb", left, right, preferred_element_type=jnp.float32)


def outer_sum(left, right):
    return jnp.einsum("ta,tb->ab", left, right, preferred_element_type=jnp.float32)


def blocks(gradient, parts_rows, parts_kc):
    height, breadth = gradient.shape
    tiled = gradient.reshape(parts_rows, height // parts_rows, parts_kc, breadth // parts_kc)
    return tiled.transpose(0, 2, 1, 3).reshape(
        parts_rows * parts_kc, height // parts_rows, breadth // parts_kc
    )


def gain_slots(gains, parts_rows, parts_kc):
    width = gains.shape[1]
    spread = gains.reshape(2, parts_rows, width // parts_rows).transpose(1, 0, 2)[:, None]
    spread = jnp.broadcast_to(spread, (parts_rows, parts_kc, 2, width // parts_rows))
    return spread.reshape(parts_rows * parts_kc, 2, width // parts_rows)


def local(
    inputs,
    w_query,
    w_key,
    w_value,
    w_out,
    w_up,
    w_down,
    gain_attn,
    gain_ffn,
    proj_e,
    lengths,
    cotangent,
):
    batches, tok_rows, width = inputs.shape
    heads = width // HEAD
    scale = HEAD ** (-0.5)
    parts_rows = lax.axis_size("rows")
    parts_kc = lax.axis_size("kc")
    column = lax.axis_index("kc")
    seq_len = tok_rows * parts_kc
    k_block = proj_e.shape[1]
    pick = (jnp.arange(parts_kc) == column).astype(jnp.float32)
    totals = None
    out_list = []
    grad_list = []
    for batch_idx in range(batches):
        length = lengths[batch_idx, 0]
        x_rows = inputs[batch_idx].astype(jnp.float32)
        h_low = normed(x_rows, gain_attn).astype(jnp.bfloat16)
        query = times_plain(h_low, w_query).astype(jnp.bfloat16)
        key_rows = times_plain(h_low, w_key).astype(jnp.bfloat16)
        value_rows = times_plain(h_low, w_value).astype(jnp.bfloat16)
        q_all, k_all, v_all = (
            lax.all_gather(query, "kc", axis=0, tiled=True),
            lax.all_gather(key_rows, "kc", axis=0, tiled=True),
            lax.all_gather(value_rows, "kc", axis=0, tiled=True),
        )
        valid = (jnp.arange(seq_len) < length).astype(jnp.float32)
        e_mask = (proj_e.astype(jnp.float32) * valid[:, None]).astype(jnp.bfloat16)
        k_comp = outer_sum(e_mask, k_all).astype(jnp.bfloat16)
        v_comp = outer_sum(e_mask, v_all).astype(jnp.bfloat16)
        q_heads = q_all.reshape(seq_len, heads, HEAD)
        kc_heads = k_comp.reshape(k_block, heads, HEAD)
        vc_heads = v_comp.reshape(k_block, heads, HEAD)
        scores = (
            jnp.einsum("qhd,khd->hqk", q_heads, kc_heads, preferred_element_type=jnp.float32)
            * scale
        )
        top = lax.pmax(jnp.max(scores, axis=-1), "kc")
        expo = jnp.exp(scores - top[:, :, None])
        total = lax.psum(jnp.sum(expo, axis=-1), "kc")
        probs = expo / total[:, :, None]
        p_low = probs.astype(jnp.bfloat16)
        o_part = jnp.einsum(
            "hqk,khd->qhd", p_low, vc_heads, preferred_element_type=jnp.float32
        ).reshape(seq_len, width)
        attended = lax.psum_scatter(
            o_part.astype(jnp.bfloat16), "kc", scatter_dimension=0, tiled=True
        )
        mid_rows = x_rows + times_plain(attended, w_out)
        h2_low = normed(mid_rows, gain_ffn).astype(jnp.bfloat16)
        up_rows = times_plain(h2_low, w_up)
        act_low = jax.nn.gelu(up_rows).astype(jnp.bfloat16)
        out_list.append((mid_rows + times_plain(act_low, w_down)).astype(jnp.bfloat16))
        cot_low = cotangent[batch_idx]
        g_down = outer_sum(act_low, cot_low)
        d_act = times_trans(cot_low, w_down)
        d_up = jax.vjp(jax.nn.gelu, up_rows)[1](d_act)[0].astype(jnp.bfloat16)
        g_up = outer_sum(h2_low, d_up)
        d_h2 = times_trans(d_up, w_up)
        d_mid_part, d_gain_ffn = jax.vjp(normed, mid_rows, gain_ffn)[1](d_h2)
        d_mid = cot_low.astype(jnp.float32) + d_mid_part
        d_attn = d_mid.astype(jnp.bfloat16)
        g_out = outer_sum(attended, d_attn)
        d_attended = times_trans(d_attn, w_out).astype(jnp.bfloat16)
        do_all = lax.all_gather(d_attended, "kc", axis=0, tiled=True)
        do_heads = do_all.reshape(seq_len, heads, HEAD)
        d_probs = jnp.einsum("qhd,khd->hqk", do_heads, vc_heads, preferred_element_type=jnp.float32)
        inner = lax.psum(jnp.sum(probs * d_probs, axis=-1), "kc")
        d_scores = (probs * (d_probs - inner[:, :, None])).astype(jnp.bfloat16)
        d_vc = (
            jnp.einsum("hqk,qhd->khd", p_low, do_heads, preferred_element_type=jnp.float32)
            .reshape(k_block, width)
            .astype(jnp.bfloat16)
        )
        d_kc = (
            (
                jnp.einsum("hqk,qhd->khd", d_scores, q_heads, preferred_element_type=jnp.float32)
                * scale
            )
            .reshape(k_block, width)
            .astype(jnp.bfloat16)
        )
        dq_part = (
            jnp.einsum("hqk,khd->qhd", d_scores, kc_heads, preferred_element_type=jnp.float32)
            * scale
        ).reshape(seq_len, width)
        d_query, d_key, d_value = (
            lax.psum_scatter(
                dq_part.astype(jnp.bfloat16), "kc", scatter_dimension=0, tiled=True
            ).astype(jnp.float32),
            lax.psum_scatter(
                times_plain(e_mask, d_kc).astype(jnp.bfloat16),
                "kc",
                scatter_dimension=0,
                tiled=True,
            ).astype(jnp.float32),
            lax.psum_scatter(
                times_plain(e_mask, d_vc).astype(jnp.bfloat16),
                "kc",
                scatter_dimension=0,
                tiled=True,
            ).astype(jnp.float32),
        )
        d_e = valid[:, None] * (times_trans(k_all, d_kc) + times_trans(v_all, d_vc))
        e_slots = (
            d_e.reshape(parts_rows, 1, seq_len // parts_rows, k_block) * pick[None, :, None, None]
        ).reshape(parts_rows * parts_kc, seq_len // parts_rows, k_block)
        dq_low = d_query.astype(jnp.bfloat16)
        dk_low = d_key.astype(jnp.bfloat16)
        dv_low = d_value.astype(jnp.bfloat16)
        g_query = outer_sum(h_low, dq_low)
        g_key = outer_sum(h_low, dk_low)
        g_value = outer_sum(h_low, dv_low)
        d_h = (
            times_trans(dq_low, w_query) + times_trans(dk_low, w_key) + times_trans(dv_low, w_value)
        )
        d_in_part, d_gain_attn = jax.vjp(normed, x_rows, gain_attn)[1](d_h)
        grad_list.append((d_mid + d_in_part).astype(jnp.bfloat16))
        gains = jnp.stack([d_gain_attn, d_gain_ffn])
        reduced = (g_query, g_key, g_value, g_out, g_up, g_down, gains, e_slots)
        if totals is None:
            totals = reduced
        else:
            totals = tuple(
                (left + right for position, (left, right) in enumerate(zip(totals, reduced)))
            )
    slotted = tuple((blocks(matrix, parts_rows, parts_kc) for matrix in totals[:6])) + (
        gain_slots(totals[6], parts_rows, parts_kc),
        totals[7],
    )
    totals = lax.psum_scatter(slotted, ("rows", "kc"), scatter_dimension=0, tiled=True)
    return (
        jnp.stack(out_list),
        jnp.stack(grad_list),
        totals[0][0],
        totals[1][0],
        totals[2][0],
        totals[3][0],
        totals[4][0],
        totals[5][0],
        totals[6][0][0],
        totals[6][0][1],
        totals[7][0],
    )


def solution(mesh):
    placed = (
        P(None, ("rows", "kc"), None),
        P(),
        P(),
        P(),
        P(),
        P(),
        P(),
        P(),
        P(),
        P(None, "kc"),
        P(None, "rows"),
        P(None, ("rows", "kc"), None),
    )
    return jax.shard_map(
        local,
        mesh=mesh,
        in_specs=placed,
        out_specs=(
            P(None, ("rows", "kc"), None),
            P(None, ("rows", "kc"), None),
            P("rows", "kc"),
            P("rows", "kc"),
            P("rows", "kc"),
            P("rows", "kc"),
            P("rows", "kc"),
            P("rows", "kc"),
            P("rows"),
            P("rows"),
            P("rows", "kc"),
        ),
        check_vma=False,
    )
```

profile of v0, /device:TPU:0, one launch (start us, length us, event | category | flops | bytes accessed | tf_op | source)
XLA Modules:
  0.0 1604.2 jit_solution(9051450450029336949)
XLA Ops:
  22.2 16.2 %all_gather.50 = bf16[256,768]{1,0:T(8,128)(2,1)S(1)} all-gather(bf16[64,768]{1,0:T(8,128)(2,1)S(1)} %convolution_convert_fusion.29), channel_id=1, replica_groups=mesh['rows'=8,'kc'=4] {'kc'}, dimensions={0}, use_global_device_ids=true | all-gather | bytes 491520 | tf_op jit(solution)/shard_map/all_gather | solution.py:79
  40.2 15.4 all_gather.57
  57.5 15.3 all_gather.59
  74.0 14.5 all_gather.56
  90.3 15.6 all_gather.49
  106.0 15.5 all_gather.58
  122.4 16.0 all_gather.55
  145.3 19.0 %all-reduce.3 = (f32[12,256]{1,0:T(8,128)S(1)}, f32[12,256]{1,0:T(8,128)S(1)}, f32[12,256]{1,0:T(8,128)S(1)}) all-reduce(f32[12,256]{1,0:T(8,128)S(1)} %get-tuple-element.81, f32[12,256]{1,0:T(8,128)S(1)} %get-tuple-element.83, f32[12,256]{1,0:T(8,128)S(1)} %get-tuple-element.85), channel_id=1, replica_groups=mesh['rows'=8,'kc'=4] {'kc'}, use_global_device_ids=true, to_apply=%region_30.0 | all-reduce | flops 9216 | bytes 73728 | tf_op jit(solution)/shard_map/pmax | solution.py:93
  168.3 17.1 %all-reduce.2 = (f32[12,256]{1,0:T(8,128)}, f32[12,256]{1,0:T(8,128)}, f32[12,256]{1,0:T(8,128)}) all-reduce(f32[12,256]{1,0:T(8,128)S(1)} %fusion.58, f32[12,256]{1,0:T(8,128)S(1)} %fusion.56, f32[12,256]{1,0:T(8,128)S(1)} %fusion.52), channel_id=1, replica_groups=mesh['rows'=8,'kc'=4] {'kc'}, use_global_device_ids=true, to_apply=%region_32.0 | all-reduce | flops 9216 | bytes 73728 | tf_op jit(solution)/shard_map/psum | solution.py:95
  188.3 15.1 all_gather.54
  207.5 16.0 all_gather.48
  238.3 13.3 reduce-scatter.70.cloned.1.call-done
  276.3 14.8 all_gather.63
  295.1 15.1 all_gather.60
  313.9 14.5 all_gather.62
  332.0 16.4 %all-reduce.1 = (f32[12,256]{1,0:T(8,128)S(1)}, f32[12,256]{1,0:T(8,128)S(1)}, f32[12,256]{1,0:T(8,128)S(1)}) all-reduce(f32[12,256]{1,0:T(8,128)S(1)} %copy-done.180, f32[12,256]{1,0:T(8,128)S(1)} %copy-done.179, f32[12,256]{1,0:T(8,128)S(1)} %get-tuple-element.98), channel_id=1, replica_groups=mesh['rows'=8,'kc'=4] {'kc'}, use_global_device_ids=true, to_apply=%region_39.0 | all-reduce | flops 9216 | bytes 73728 | tf_op jit(solution)/shard_map/psum | solution.py:123
  388.3 6.7 reduce-scatter.78.cloned.1.call-done
  397.0 19.0 %reduce-scatter.84.cloned.1.call-done = bf16[64,768]{1,0:T(8,128)(2,1)} async-done(((bf16[256,768]{1,0:T(8,128)(2,1)}), bf16[64,768]{1,0:T(8,128)(2,1)}) %reduce-scatter.84.cloned.1.call-update) | async-done | bytes 98320
  418.1 19.7 %reduce-scatter.52.cloned.1.call-done = bf16[64,768]{1,0:T(8,128)(2,1)} async-done(((bf16[256,768]{1,0:T(8,128)(2,1)}), bf16[64,768]{1,0:T(8,128)(2,1)}) %reduce-scatter.52.cloned.1.call-update) | async-done | bytes 98320 | tf_op jit(solution)/shard_map/reduce_scatter | solution.py:146
  439.9 19.1 %reduce-scatter.40.cloned.1.call-done = bf16[64,768]{1,0:T(8,128)(2,1)} async-done(((bf16[256,768]{1,0:T(8,128)(2,1)}), bf16[64,768]{1,0:T(8,128)(2,1)}) %reduce-scatter.40.cloned.1.call-update) | async-done | bytes 98320 | tf_op jit(solution)/shard_map/reduce_scatter | solution.py:146
  461.2 19.0 %reduce-scatter.48.cloned.1.call-done = bf16[64,768]{1,0:T(8,128)(2,1)} async-done(((bf16[256,768]{1,0:T(8,128)(2,1)}), bf16[64,768]{1,0:T(8,128)(2,1)}) %reduce-scatter.48.cloned.1.call-update) | async-done | bytes 98320 | tf_op jit(solution)/shard_map/reduce_scatter | solution.py:146
  482.4 19.0 %reduce-scatter.50.cloned.1.call-done = bf16[64,768]{1,0:T(8,128)(2,1)} async-done(((bf16[256,768]{1,0:T(8,128)(2,1)}), bf16[64,768]{1,0:T(8,128)(2,1)}) %reduce-scatter.50.cloned.1.call-update) | async-done | bytes 98320 | tf_op jit(solution)/shard_map/reduce_scatter | solution.py:152
  503.5 19.0 %reduce-scatter.54.cloned.1.call-done = bf16[64,768]{1,0:T(8,128)(2,1)} async-done(((bf16[256,768]{1,0:T(8,128)(2,1)}), bf16[64,768]{1,0:T(8,128)(2,1)}) %reduce-scatter.54.cloned.1.call-update) | async-done | bytes 98320 | tf_op jit(solution)/shard_map/reduce_scatter | solution.py:152
  524.7 19.5 %reduce-scatter.42.cloned.1.call-done = bf16[64,768]{1,0:T(8,128)(2,1)} async-done(((bf16[256,768]{1,0:T(8,128)(2,1)}), bf16[64,768]{1,0:T(8,128)(2,1)}) %reduce-scatter.42.cloned.1.call-update) | async-done | bytes 98320 | tf_op jit(solution)/shard_map/reduce_scatter | solution.py:152
  551.5 14.8 all_gather.51
  568.2 15.3 all_gather.53
  584.6 14.4 all_gather.52
  601.3 15.6 pmax.29
  617.0 16.3 %psum.57 = f32[12,256]{1,0:T(8,128)S(1)} all-reduce(f32[12,256]{1,0:T(8,128)S(1)} %fusion.54), channel_id=1, replica_groups=mesh['rows'=8,'kc'=4] {'kc'}, use_global_device_ids=true, to_apply=%region_14.0 | all-reduce | flops 3072 | bytes 24576 | tf_op jit(solution)/shard_map/psum | solution.py:95
  645.2 10.7 reduce-scatter.72.cloned.1.call-done
  668.7 14.7 all_gather.61
  690.2 15.8 psum.61
  810.8 5.2 fusion.142
  815.9 11.1 add_add_fusion
  827.1 9.7 copy.154
  836.7 5.9 copy.177
  842.6 5.4 copy.155
  851.6 5.1 fusion.201
  861.8 12.1 add_add_fusion.1
  873.9 12.4 reshape.466
  886.3 8.9 copy.153
  915.7 38.8 %all-reduce = f32[32,2,96]{2,1,0:T(2,128)S(1)} all-reduce(f32[32,2,96]{2,1,0:T(2,128)S(1)} %bitcast.541), channel_id=24, replica_groups=mesh['rows'=8,'kc'=4] {'rows','kc'}, use_global_device_ids=true, to_apply=%region_86.0.clone | all-reduce | flops 6144 | bytes 49152
  957.4 34.5 %reduce-scatter.62.cloned.1.call-done = f32[1,96,192]{2,1,0:T(8,128)} async-done(((f32[32,96,192]{2,1,0:T(8,128)}), f32[1,96,192]{2,1,0:T(8,128)}) %reduce-scatter.62.cloned.1.call-update) | async-done | bytes 73744 | tf_op jit(solution)/shard_map/reduce_scatter | solution.py:186
  991.9 107.4 %reduce-scatter.60.cloned.1.call-done = f32[1,96,192]{2,1,0:T(8,128)} async-done(((f32[32,96,192]{2,1,0:T(8,128)}), f32[1,96,192]{2,1,0:T(8,128)}) %reduce-scatter.60.cloned.1.call-update) | async-done | bytes 73744 | tf_op jit(solution)/shard_map/reduce_scatter | solution.py:186
  1099.3 107.3 %reduce-scatter.58.cloned.1.call-done = f32[1,96,192]{2,1,0:T(8,128)} async-done(((f32[32,96,192]{2,1,0:T(8,128)}), f32[1,96,192]{2,1,0:T(8,128)}) %reduce-scatter.58.cloned.1.call-update) | async-done | bytes 73744 | tf_op jit(solution)/shard_map/reduce_scatter | solution.py:186
  1206.6 107.4 %reduce-scatter.56.cloned.1.call-done = f32[1,96,192]{2,1,0:T(8,128)} async-done(((f32[32,96,192]{2,1,0:T(8,128)}), f32[1,96,192]{2,1,0:T(8,128)}) %reduce-scatter.56.cloned.1.call-update) | async-done | bytes 73744 | tf_op jit(solution)/shard_map/reduce_scatter | solution.py:186
  1314.0 142.0 %reduce-scatter.66.cloned.1.call-done = f32[1,384,192]{1,2,0:T(8,128)} async-done(((f32[32,384,192]{1,2,0:T(8,128)}), f32[1,384,192]{1,2,0:T(8,128)}) %reduce-scatter.66.cloned.1.call-update) | async-done | bytes 294928 | tf_op jit(solution)/shard_map/reduce_scatter | solution.py:186
  1456.0 141.3 %reduce-scatter.64.cloned.1.call-done = f32[1,96,768]{2,1,0:T(8,128)} async-done(((f32[32,96,768]{2,1,0:T(8,128)}), f32[1,96,768]{2,1,0:T(8,128)}) %reduce-scatter.64.cloned.1.call-update) | async-done | bytes 294928 | tf_op jit(solution)/shard_map/reduce_scatter | solution.py:186
  (736 shorter events, 324.0 us)
Async XLA Ops:
  7.2 224.3 %reduce-scatter.76.cloned.1.call-start = ((), (), s32[]{:S(2)}) async-start(), calls=%async_computation.41 | async-start | bytes 491520
  9.2 197.9 %copy-start.138 = (f32[64]{0:T(128)}, f32[64]{0:T(128)S(1)}, u32[]{:S(2)}) copy-start(f32[64]{0:T(128)S(1)} %broadcast_multiply_fusion.7) | copy-start | bytes 772
  19.2 37.2 %copy-start.34 = (bf16[256,64]{0,1:T(8,128)(2,1)S(1)}, bf16[256,64]{0,1:T(8,128)(2,1)}, u32[]{:S(2)}) copy-start(bf16[256,64]{0,1:T(8,128)(2,1)} %param.21) | copy-start | bytes 98308
  19.2 38.3 %copy-start.120 = (bf16[64,768]{1,0:T(8,128)(2,1)S(1)}, bf16[64,768]{1,0:T(8,128)(2,1)}, u32[]{:S(2)}) copy-start(bf16[64,768]{1,0:T(8,128)(2,1)} %convolution_convert_fusion.20) | copy-start | bytes 294916
  20.5 53.3 %copy-start.154 = (f32[256]{0:T(256)}, f32[256]{0:T(256)S(1)}, u32[]{:S(2)}) copy-start(f32[256]{0:T(256)S(1)} %compare_convert_fusion.4) | copy-start | bytes 3076
  21.1 52.6 %copy-start.147 = (f32[256]{0:T(256)}, f32[256]{0:T(256)S(1)}, u32[]{:S(2)}) copy-start(f32[256]{0:T(256)S(1)} %compare_convert_fusion.1) | copy-start | bytes 3076
  21.8 66.7 %copy-start.150 = (f32[256]{0:T(256)}, f32[256]{0:T(256)S(1)}, u32[]{:S(2)}) copy-start(f32[256]{0:T(256)S(1)} %compare_convert_fusion.2) | copy-start | bytes 3076
  21.8 52.1 %copy-start.118 = (bf16[64,768]{1,0:T(8,128)(2,1)S(1)}, bf16[64,768]{1,0:T(8,128)(2,1)}, u32[]{:S(2)}) copy-start(bf16[64,768]{1,0:T(8,128)(2,1)} %convolution_convert_fusion.23) | copy-start | bytes 294916
  39.2 51.1 %copy-start.119 = (bf16[64,768]{1,0:T(8,128)(2,1)S(1)}, bf16[64,768]{1,0:T(8,128)(2,1)}, u32[]{:S(2)}) copy-start(bf16[64,768]{1,0:T(8,128)(2,1)} %convolution_convert_fusion.30) | copy-start | bytes 294916
  73.9 68.0 %copy-start.82 = (bf16[64,768]{0,1:T(8,128)(2,1)}, bf16[64,768]{0,1:T(8,128)(2,1)S(1)}, u32[]{:S(2)}) copy-start(bf16[64,768]{0,1:T(8,128)(2,1)S(1)} %copy.176) | copy-start | bytes 294916
  106.0 38.1 %copy-start.56 = (bf16[256,768]{0,1:T(8,128)(2,1)}, bf16[256,768]{0,1:T(8,128)(2,1)S(1)}, u32[]{:S(2)}) copy-start(bf16[256,768]{0,1:T(8,128)(2,1)S(1)} %copy.125) | copy-start | bytes 1179652
  144.1 41.2 %copy-start.129 = (bf16[64,12,64]{2,1,0:T(8,128)(2,1)S(1)}, bf16[64,12,64]{2,1,0:T(8,128)(2,1)}, u32[]{:S(2)}) copy-start(bf16[64,12,64]{2,1,0:T(8,128)(2,1)} %reshape.451) | copy-start | bytes 294916
  164.4 40.1 %copy-start.136 = (f32[12,256]{1,0:T(8,128)}, f32[12,256]{1,0:T(8,128)S(1)}, u32[]{:S(2)}) copy-start(f32[12,256]{1,0:T(8,128)S(1)} %get-tuple-element.50) | copy-start | bytes 36868
  187.8 46.5 %reduce-scatter.74.cloned.1.call-start = ((), (), s32[]{:S(2)}) async-start(), calls=%async_computation.40 | async-start | bytes 491520
  207.1 44.6 %reduce-scatter.70.cloned.1.call-start = ((), (), s32[]{:S(2)}) async-start(), calls=%async_computation.38 | async-start | bytes 491520
  231.3 154.9 %reduce-scatter.82.cloned.1.call-start = ((), (), s32[]{:S(2)}) async-start(), calls=%async_computation.44 | async-start | bytes 491520
  353.7 41.2 %reduce-scatter.78.cloned.1.call-start = ((), (), s32[]{:S(2)}) async-start(), calls=%async_computation.42 | async-start | bytes 491520
  359.8 56.2 %reduce-scatter.84.cloned.1.call-start = ((), (), s32[]{:S(2)}) async-start(), calls=%async_computation.45 | async-start | bytes 491520
  365.0 72.8 %reduce-scatter.52.cloned.1.call-start = ((), (), s32[]{:S(2)}) async-start(), calls=%async_computation.29 | async-start | bytes 491520 | tf_op jit(solution)/shard_map/reduce_scatter | solution.py:146
  367.5 91.5 %reduce-scatter.40.cloned.1.call-start = ((), (), s32[]{:S(2)}) async-start(), calls=%async_computation.23 | async-start | bytes 491520 | tf_op jit(solution)/shard_map/reduce_scatter | solution.py:146
  370.7 109.6 %reduce-scatter.48.cloned.1.call-start = ((), (), s32[]{:S(2)}) async-start(), calls=%async_computation.27 | async-start | bytes 491520 | tf_op jit(solution)/shard_map/reduce_scatter | solution.py:146
  373.9 127.5 %reduce-scatter.50.cloned.1.call-start = ((), (), s32[]{:S(2)}) async-start(), calls=%async_computation.28 | async-start | bytes 491520 | tf_op jit(solution)/shard_map/reduce_scatter | solution.py:152
  376.5 146.0 %reduce-scatter.54.cloned.1.call-start = ((), (), s32[]{:S(2)}) async-start(), calls=%async_computation.30 | async-start | bytes 491520 | tf_op jit(solution)/shard_map/reduce_scatter | solution.py:152
  379.6 164.6 %reduce-scatter.42.cloned.1.call-start = ((), (), s32[]{:S(2)}) async-start(), calls=%async_computation.24 | async-start | bytes 491520 | tf_op jit(solution)/shard_map/reduce_scatter | solution.py:152
  386.1 269.8 %reduce-scatter.72.cloned.1.call-start = ((), (), s32[]{:S(2)}) async-start(), calls=%async_computation.39 | async-start | bytes 491520
  601.2 34.1 %copy-start.41 = (f32[12,256,64]{1,2,0:T(8,128)}, f32[12,256,64]{1,2,0:T(8,128)S(1)}, u32[]{:S(2)}) copy-start(f32[12,256,64]{1,2,0:T(8,128)S(1)} %get-tuple-element.102) | copy-start | bytes 2359300
  637.3 112.2 %reduce-scatter.46.cloned.1.call-start = ((), (), s32[]{:S(2)}) async-start(), calls=%async_computation.26 | async-start | bytes 491520 | tf_op jit(solution)/shard_map/reduce_scatter | solution.py:152
  668.1 62.0 %copy-start.66 = (f32[64,768]{1,0:T(8,128)}, f32[64,768]{1,0:T(8,128)S(1)}, u32[]{:S(2)}) copy-start(f32[64,768]{1,0:T(8,128)S(1)} %get-tuple-element.53) | copy-start | bytes 589828
  687.7 81.1 %reduce-scatter.44.cloned.1.call-start = ((), (), s32[]{:S(2)}) async-start(), calls=%async_computation.25 | async-start | bytes 491520 | tf_op jit(solution)/shard_map/reduce_scatter | solution.py:146
  711.3 76.9 %reduce-scatter.80.cloned.1.call-start = ((), (), s32[]{:S(2)}) async-start(), calls=%async_computation.43 | async-start | bytes 491520
  720.4 237.0 %reduce-scatter.68.cloned.1.call-start = ((), (), s32[]{:S(2)}) async-start(), calls=%async_computation.37 | async-start | bytes 540672 | tf_op jit(solution)/shard_map/reduce_scatter | solution.py:186
  730.0 261.8 %reduce-scatter.62.cloned.1.call-start = ((), (), s32[]{:S(2)}) async-start(), calls=%async_computation.34 | async-start | bytes 3244032 | tf_op jit(solution)/shard_map/reduce_scatter | solution.py:186
  744.7 354.6 %reduce-scatter.60.cloned.1.call-start = ((), (), s32[]{:S(2)}) async-start(), calls=%async_computation.33 | async-start | bytes 3244032 | tf_op jit(solution)/shard_map/reduce_scatter | solution.py:186
  764.0 442.6 %reduce-scatter.58.cloned.1.call-start = ((), (), s32[]{:S(2)}) async-start(), calls=%async_computation.32 | async-start | bytes 3244032 | tf_op jit(solution)/shard_map/reduce_scatter | solution.py:186
  783.4 530.6 %reduce-scatter.56.cloned.1.call-start = ((), (), s32[]{:S(2)}) async-start(), calls=%async_computation.31 | async-start | bytes 3244032 | tf_op jit(solution)/shard_map/reduce_scatter | solution.py:186
  802.8 653.2 %reduce-scatter.66.cloned.1.call-start = ((), (), s32[]{:S(2)}) async-start(), calls=%async_computation.36 | async-start | bytes 9732096 | tf_op jit(solution)/shard_map/reduce_scatter | solution.py:186
  848.1 749.1 %reduce-scatter.64.cloned.1.call-start = ((), (), s32[]{:S(2)}) async-start(), calls=%async_computation.35 | async-start | bytes 9732096 | tf_op jit(solution)/shard_map/reduce_scatter | solution.py:186
  912.0 42.6 %copy-start.48 = (bf16[4,64,768]{2,1,0:T(8,128)(2,1)S(1)}, bf16[4,64,768]{2,1,0:T(8,128)(2,1)}, u32[]{:S(2)}) copy-start(bf16[4,64,768]{2,1,0:T(8,128)(2,1)} %param.23) | copy-start | bytes 1179652
  912.0 42.6 %copy-start.198 = (f32[64]{0:T(128)S(1)}, f32[64]{0:T(128)}, u32[]{:S(2)}) copy-start(f32[64]{0:T(128)} %copy-done.196) | copy-start | bytes 772
  912.0 42.6 %copy-start.204 = (f32[64]{0:T(128)S(1)}, f32[64]{0:T(128)}, u32[]{:S(2)}) copy-start(f32[64]{0:T(128)} %copy-done.203) | copy-start | bytes 772
  912.5 42.1 %copy-start.67 = (f32[64,768]{1,0:T(8,128)S(1)}, f32[64,768]{1,0:T(8,128)}, u32[]{:S(2)}) copy-start(f32[64,768]{1,0:T(8,128)} %copy-done.66) | copy-start | bytes 589828
  912.5 42.1 %copy-start.76 = (f32[64,768]{1,0:T(8,128)S(1)}, f32[64,768]{1,0:T(8,128)}, u32[]{:S(2)}) copy-start(f32[64,768]{1,0:T(8,128)} %copy-done.75) | copy-start | bytes 589828
  912.5 42.1 %copy-start.100 = (f32[64,768]{1,0:T(8,128)S(1)}, f32[64,768]{1,0:T(8,128)}, u32[]{:S(2)}) copy-start(f32[64,768]{1,0:T(8,128)} %get-tuple-element.100) | copy-start | bytes 589828
  912.5 43.3 %copy-start.70 = (f32[64,768]{1,0:T(8,128)S(1)}, f32[64,768]{1,0:T(8,128)}, u32[]{:S(2)}) copy-start(f32[64,768]{1,0:T(8,128)} %convolution_add_fusion) | copy-start | bytes 589828
  912.6 43.3 %copy-start.72 = (f32[64,768]{1,0:T(8,128)S(1)}, f32[64,768]{1,0:T(8,128)}, u32[]{:S(2)}) copy-start(f32[64,768]{1,0:T(8,128)} %copy-done.71) | copy-start | bytes 589828
  912.6 43.3 %copy-start.74 = (f32[64,768]{1,0:T(8,128)S(1)}, f32[64,768]{1,0:T(8,128)}, u32[]{:S(2)}) copy-start(f32[64,768]{1,0:T(8,128)} %copy-done.73) | copy-start | bytes 589828
  912.6 43.3 %copy-start.200 = (f32[64]{0:T(128)S(1)}, f32[64]{0:T(128)}, u32[]{:S(2)}) copy-start(f32[64]{0:T(128)} %copy-done.199) | copy-start | bytes 772
  912.6 43.3 %copy-start.202 = (f32[64]{0:T(128)S(1)}, f32[64]{0:T(128)}, u32[]{:S(2)}) copy-start(f32[64]{0:T(128)} %copy-done.201) | copy-start | bytes 772
  (203 other events, 1373.3 us)
Sparse Core Ops, SparseCore 0:
  187.9 20.9 reduce-scatter.75
  211.3 18.9 reduce-scatter.73
  232.7 18.8 reduce-scatter.69
  353.9 20.0 reduce-scatter.81
  376.1 18.8 reduce-scatter.77
  397.2 18.8 reduce-scatter.83
  418.9 18.8 reduce-scatter.51
  440.1 18.8 reduce-scatter.39
  461.3 18.8 reduce-scatter.47
  482.5 18.8 reduce-scatter.49
  503.6 18.8 reduce-scatter.53
  525.3 18.8 reduce-scatter.41
  637.4 18.4 reduce-scatter.71
  687.9 18.8 reduce-scatter.45
  711.4 18.9 reduce-scatter.43
  733.3 18.8 reduce-scatter.79
  754.8 132.7 reduce-scatter.67
  894.3 97.5 reduce-scatter.61
  998.8 100.4 reduce-scatter.59
  1106.0 100.5 reduce-scatter.57
  1213.5 100.4 reduce-scatter.55
  1321.5 134.4 reduce-scatter.65
  1462.5 134.7 reduce-scatter.63
where the time goes:
time: 1610 us; the launch traced here: 1600 us
  waiting for transfers between devices  805 us (50%)
  blocking collectives  382 us (24%)
  matrix products  242 us (15%)
  local copies, waits for them, and re-layouts  128 us (8%)
  other arithmetic  27.3 us (2%)
  between operations  17.4 us (1%)
    reduce_scatter x7, waiting for transfers between devices, local(): lax.psum_scatter(slotted, ('rows', 'kc'), scatter_dimension=0, tiled=True)  640 us
    dot_general x32, matrix products, outer_sum(): jnp.einsum('ta,tb->ab', left, right, preferred_element_type=jnp.float32)  90.1 us
    all_gather x4, blocking collectives, local(): lax.all_gather(query, 'kc', axis=0, tiled=True)  61.4 us
    all_gather x4, blocking collectives, local(): lax.all_gather(value_rows, 'kc', axis=0, tiled=True)  61.3 us
    all_gather x4, blocking collectives, local(): lax.all_gather(key_rows, 'kc', axis=0, tiled=True)  61.3 us
    all_gather x4, blocking collectives, local(): do_all = lax.all_gather(d_attended, 'kc', axis=0, tiled=True)  59.2 us
    dot_general x32, matrix products, times_trans(): jnp.einsum('ta,ba->tb', left, right, preferred_element_type=jnp.float32)  58.9 us
    reduce_scatter x4, waiting for transfers between devices, local(): lax.psum_scatter(times_plain(e_mask, d_kc).astype(jnp.bfloat16), 'kc', sc...  57.8 us
  transfers between devices with their start and end apart: 23, of which 16 were waited for; matrix products, arithmetic and copies ran while one was open for 17% of the time, Pallas kernels for 0%

commit v1 on v0

v1 whole, which is shorter than its diff:
```python
import math

import jax
import jax.numpy as jnp
from jax import lax
from jax.sharding import PartitionSpec as P

HEAD = 64
BF = jnp.bfloat16
F32 = jnp.float32


def normed(values):
    centred = values - jnp.mean(values, axis=-1, keepdims=True)
    rstd = lax.rsqrt(jnp.mean(centred * centred, axis=-1, keepdims=True) + 1e-05)
    return centred * rstd, rstd


def norm_back(n, rstd, gain, d):
    dc = d * gain
    return rstd * (
        dc - jnp.mean(dc, axis=-1, keepdims=True) - n * jnp.mean(dc * n, axis=-1, keepdims=True)
    )


def mm(left, right):
    return jnp.dot(left, right, preferred_element_type=F32)


def mm_t(left, right):
    return jnp.einsum("ta,ba->tb", left, right, preferred_element_type=F32)


def t_mm(left, right):
    return jnp.einsum("ta,tb->ab", left, right, preferred_element_type=F32)


class Grid:
    def __init__(self, n_rows, n_kc):
        self.n_rows, self.n_kc = n_rows, n_kc
        self.nc = 2 if n_rows % 2 == 0 else 1
        plane = n_rows // self.nc
        self.nx = next(d for d in range(math.isqrt(plane), 0, -1) if plane % d == 0)
        self.ny = plane // self.nx
        row = lax.axis_index("rows")
        self.c = row % self.nc
        self.x = (row // self.nc) % self.nx
        self.y = row // (self.nc * self.nx)
        self.z = lax.axis_index("kc")

    def send(self, value, axis, shift):
        if axis == "z":
            n = self.n_kc
            return lax.ppermute(value, "kc", [(i, (i + shift) % n) for i in range(n)])
        pairs = []
        for i in range(self.n_rows):
            c, x, y = i % self.nc, (i // self.nc) % self.nx, i // (self.nc * self.nx)
            if axis == "c":
                c = (c + shift) % self.nc
            elif axis == "x":
                x = (x + shift) % self.nx
            else:
                y = (y + shift) % self.ny
            pairs.append((i, (y * self.nx + x) * self.nc + c))
        return lax.ppermute(value, "rows", pairs)

    def scatter_sum(self, value, dim, axis):
        n = {"c": self.nc, "x": self.nx, "y": self.ny, "z": self.n_kc}[axis]
        me = {"c": self.c, "x": self.x, "y": self.y, "z": self.z}[axis]
        total = lax.dynamic_index_in_dim(value, me, dim, keepdims=False).astype(F32)
        for shift in range(1, n):
            block = lax.dynamic_index_in_dim(value, (me + shift) % n, dim, keepdims=False)
            total = total + self.send(block, axis, shift).astype(F32)
        return total


def reduce_grad(grid, value, low=True):
    kind = BF if low else F32
    half = value.shape[2] // 2
    if half % 16:
        parts = ((value, "x"),)
    else:
        parts = ((value[:, :, :half], "x"), (value[:, :, half:], "y"))
    done = []
    for part, first in parts:
        part = part.astype(kind)
        if first == "x":
            part = grid.scatter_sum(part, 1, "x").astype(kind)
            part = grid.scatter_sum(part, 0, "y").astype(kind)
        else:
            part = grid.scatter_sum(part, 0, "y").astype(kind)
            part = grid.scatter_sum(part, 0, "x").astype(kind)
        done.append(grid.scatter_sum(part, 1, "z"))
    return jnp.concatenate(done, axis=0)


def local(
    inputs,
    w_query,
    w_key,
    w_value,
    w_out,
    w_up,
    w_down,
    gain_attn,
    gain_ffn,
    proj_e,
    lengths,
    cotangent,
):
    batches, t, width = inputs.shape
    heads = width // HEAD
    ff = w_up.shape[1]
    scale = HEAD ** (-0.5)
    n_rows, n_kc = lax.axis_size("rows"), lax.axis_size("kc")
    grid = Grid(n_rows, n_kc)
    share = n_kc // batches
    seq_len = proj_e.shape[0]
    mine = batches * t
    my_batch, my_part = grid.z // share, grid.z % share
    lane, part = grid.z % batches, grid.z // batches

    def reorder(got, first):
        stacked = jnp.stack(got)
        return jnp.stack(
            [
                lax.dynamic_index_in_dim(stacked, (first - i) % batches, 0, keepdims=False)
                for i in range(batches)
            ]
        )

    def gather_seq(v):
        got = []
        for j in range(batches):
            block = lax.dynamic_index_in_dim(v, (lane + j) % batches, 0, keepdims=False)
            pairs = [
                (i, ((i % batches + j) % batches) * share + i // batches) for i in range(n_kc)
            ]
            got.append(block if all(a == b for a, b in pairs) else lax.ppermute(block, "kc", pairs))
        return reorder(got, my_batch).reshape(mine, width)

    def spread_seq(v):
        blocks = v.reshape(batches, t, width)
        got = []
        for j in range(batches):
            block = lax.dynamic_index_in_dim(blocks, (my_batch - j) % batches, 0, keepdims=False)
            pairs = [
                (((i % batches + j) % batches) * share + i // batches, i) for i in range(n_kc)
            ]
            got.append(block if all(a == b for a, b in pairs) else lax.ppermute(block, "kc", pairs))
        return reorder(got[:1] + got[:0:-1], lane + batches).reshape(inputs.shape)

    def seq_sum(v):
        if share == 1:
            return v
        groups = [[b * share + p for p in range(share)] for b in range(batches)]
        return lax.psum(v, "kc", axis_index_groups=groups)

    x_low = gather_seq(inputs)
    e_t = lax.all_gather(proj_e.T, "kc", axis=0, tiled=True)
    dy = gather_seq(cotangent)
    e_t = lax.dynamic_slice_in_dim(e_t, my_part * mine, mine, 1)
    length = lax.dynamic_index_in_dim(lengths, my_batch, 0, keepdims=False)[0]
    valid = (my_part * mine + jnp.arange(mine)) < length
    e_mask = jnp.where(valid[None, :], e_t, jnp.zeros_like(e_t))

    x = x_low.astype(F32)
    n1, r1 = normed(x)
    h = (n1 * gain_attn).astype(BF)
    query, key, value = (mm(h, w).astype(BF) for w in (w_query, w_key, w_value))
    k_comp = seq_sum(mm(e_mask, key)).astype(BF)
    v_comp = seq_sum(mm(e_mask, value)).astype(BF)
    q_h = query.reshape(mine, heads, HEAD)
    kc_h = k_comp.reshape(-1, heads, HEAD)
    vc_h = v_comp.reshape(-1, heads, HEAD)
    scores = jnp.einsum("qhd,khd->hqk", q_h, kc_h, preferred_element_type=F32) * scale
    probs = jax.nn.softmax(scores, axis=-1)
    p_low = probs.astype(BF)
    attended = (
        jnp.einsum("hqk,khd->qhd", p_low, vc_h, preferred_element_type=F32)
        .reshape(mine, width)
        .astype(BF)
    )
    mid = x + mm(attended, w_out)
    n2, r2 = normed(mid)
    h2 = (n2 * gain_ffn).astype(BF)
    up = mm(h2, w_up)
    act = jax.nn.gelu(up).astype(BF)
    output = spread_seq((mid + mm(act, w_down)).astype(BF))

    nc, nx, ny = grid.nc, grid.nx, grid.ny

    def by_core(v):
        v = v.reshape(mine, ny * nx, nc, -1)
        own = lax.dynamic_index_in_dim(v, grid.c, 2, keepdims=False)
        other = lax.dynamic_index_in_dim(v, nc - 1 - grid.c, 2, keepdims=False)
        return own.reshape(mine, -1), other.reshape(mine, -1)

    def pair_grad(split, whole):
        own, other = by_core(split)
        return t_mm(own, whole) + t_mm(grid.send(other, "c", 1), grid.send(whole, "c", 1))

    g_down = pair_grad(act, dy)
    g_down = reduce_grad(grid, g_down.reshape(ny, nx, ff // n_rows, n_kc, width // n_kc))
    d_act = mm_t(dy, w_down)
    d_up = jax.vjp(jax.nn.gelu, up)[1](d_act)[0].astype(BF)
    g_up = pair_grad(h2, d_up)
    g_up = reduce_grad(grid, g_up.reshape(ny, nx, width // n_rows, n_kc, ff // n_kc))
    d_h2 = mm_t(d_up, w_up)
    gg_ffn = jnp.sum(d_h2 * n2, axis=0)
    d_mid = dy.astype(F32) + norm_back(n2, r2, gain_ffn, d_h2)
    d_attn = d_mid.astype(BF)
    d_att = mm_t(d_attn, w_out).astype(BF)
    do_h = d_att.reshape(mine, heads, HEAD)
    d_probs = jnp.einsum("qhd,khd->hqk", do_h, vc_h, preferred_element_type=F32)
    inner = jnp.sum(probs * d_probs, axis=-1, keepdims=True)
    d_scores = (probs * (d_probs - inner)).astype(BF)
    d_vc = seq_sum(jnp.einsum("hqk,qhd->khd", p_low, do_h, preferred_element_type=F32))
    d_vc = d_vc.reshape(-1, width).astype(BF)
    d_kc = seq_sum(jnp.einsum("hqk,qhd->khd", d_scores, q_h, preferred_element_type=F32) * scale)
    d_kc = d_kc.reshape(-1, width).astype(BF)
    d_query = jnp.einsum("hqk,khd->qhd", d_scores, kc_h, preferred_element_type=F32) * scale
    d_query = d_query.reshape(mine, width).astype(BF)
    d_key = t_mm(e_mask, d_kc).astype(BF)
    d_value = t_mm(e_mask, d_vc).astype(BF)
    d_e = jnp.where(valid[:, None], mm_t(key, d_kc) + mm_t(value, d_vc), 0.0)
    attn = []
    for split, whole in ((h, d_query), (h, d_key), (h, d_value), (attended, d_attn)):
        g = pair_grad(split, whole)
        attn.append(reduce_grad(grid, g.reshape(ny, nx, width // n_rows, n_kc, width // n_kc)))
    d_h = mm_t(d_query, w_query) + mm_t(d_key, w_key) + mm_t(d_value, w_value)
    gg_attn = jnp.sum(d_h * n1, axis=0)
    grad_in = spread_seq((d_mid + norm_back(n1, r1, gain_attn, d_h)).astype(BF))

    if share > 1:
        d_e = lax.dynamic_update_slice(
            jnp.zeros((seq_len, d_e.shape[1]), F32), d_e, (my_part * mine, 0)
        )
    e_rows, e_cols = seq_len // n_rows, d_e.shape[1] // n_kc
    d_e = d_e.reshape(n_rows, e_rows, n_kc, e_cols).transpose(0, 2, 1, 3)
    g_cols = width // n_rows
    gains = jnp.stack([gg_attn, gg_ffn]).reshape(2, n_rows, g_cols).transpose(1, 0, 2)
    gains = jnp.broadcast_to(gains[:, None], (n_rows, n_kc, 2, g_cols))
    small = jnp.concatenate(
        [d_e.reshape(n_rows, n_kc, -1), gains.reshape(n_rows, n_kc, -1)], axis=2
    )
    small = small.reshape(ny, nx, nc, n_kc, -1)
    if nc > 1:
        small = grid.scatter_sum(small, 2, "c")
    small = grid.scatter_sum(small, 1, "x")
    small = grid.scatter_sum(small, 0, "y")
    small = grid.scatter_sum(small, 0, "z")
    n_e = e_rows * e_cols
    return (
        output,
        grad_in,
        attn[0],
        attn[1],
        attn[2],
        attn[3],
        g_up,
        g_down,
        small[n_e : n_e + g_cols],
        small[n_e + g_cols :],
        small[:n_e].reshape(e_rows, e_cols),
    )


def solution(mesh):
    tokens = P(None, ("rows", "kc"), None)
    return jax.shard_map(
        local,
        mesh=mesh,
        in_specs=(tokens,) + (P(),) * 8 + (P(None, "kc"), P(None, "rows"), tokens),
        out_specs=(tokens, tokens) + (P("rows", "kc"),) * 6 + (P("rows"), P("rows"))
        + (P("rows", "kc"),),
        check_vma=False,
    )
```

time: 1610 us -> 371 us (0.23)
  waiting for transfers between devices: 805 us -> 66.4 us
  blocking collectives: 382 us -> 16.6 us
  matrix products: 242 us -> 73.6 us
  starting transfers between devices: 2.17 us -> 101 us
  local copies, waits for them, and re-layouts: 128 us -> 79.2 us
    reduce_scatter x15 -> x0, waiting for transfers between devices: 755 us -> none  [the longest x7 640 us: local(): lax.psum_scatter(slotted, ('rows', 'kc'), scatter_dimension=0, tiled=True)]
    all_gather x16 -> x1, blocking collectives: 243 us -> 16.6 us  [local(): e_t = lax.all_gather(proj_e.T, 'kc', axis=0, tiled=True)]
    dot_general x120 -> x35, matrix products: 242 us -> 70.7 us  [the longest x14 32.3 us: t_mm(): return jnp.einsum('ta,tb->ab', left, right, preferred_element_type=F32)]
    ppermute x0 -> x88, starting transfers between devices: none -> 101 us  [the longest x39 47.6 us: send(): return lax.ppermute(value, 'kc', [(i, (i + shift) % n) for i in range(n)])]
    ppermute x0 -> x88, waiting for transfers between devices: none -> 66.4 us  [the longest x39 34.5 us: send(): return lax.ppermute(value, 'kc', [(i, (i + shift) % n) for i in range(n)])]
    psum x4 -> x0, blocking collectives: 65.5 us -> none  [the longest x2 33.4 us: local(): total = lax.psum(jnp.sum(expo, axis=-1), 'kc')]
    unnamed x31 -> x0, waiting for transfers between devices: 50.1 us -> none
    unnamed x1 -> x0, blocking collectives: 38.8 us -> none
  transfers between devices with their start and end apart: 23 -> 88, of which waited for: 16 -> 41; matrix products, arithmetic and copies ran while one was open for 17% -> 39% of each run, Pallas kernels for 0% -> 0%
where the time goes in v1:
time: 371 us; the launch traced here: 364 us
  starting transfers between devices  101 us (27%)
  local copies, waits for them, and re-layouts  79.2 us (21%)
  matrix products  73.6 us (20%)
  waiting for transfers between devices  66.4 us (18%)
  other arithmetic  24.3 us (7%)
  blocking collectives  16.6 us (4%)
    ppermute x39, starting transfers between devices, send(): return lax.ppermute(value, 'kc', [(i, (i + shift) % n) for i in range(n)])  47.6 us
    ppermute x39, waiting for transfers between devices, send(): return lax.ppermute(value, 'kc', [(i, (i + shift) % n) for i in range(n)])  34.5 us
    ppermute x37, starting transfers between devices, send(): return lax.ppermute(value, 'rows', pairs)  34.1 us
    dot_general x14, matrix products, t_mm(): return jnp.einsum('ta,tb->ab', left, right, preferred_element_type=F32)  32.3 us
    ppermute x37, waiting for transfers between devices, send(): return lax.ppermute(value, 'rows', pairs)  26.3 us
    another operation x7, local copies, waits for them, and re-layouts  18.1 us
    all_gather x1, blocking collectives, local(): e_t = lax.all_gather(proj_e.T, 'kc', axis=0, tiled=True)  16.6 us
    dot_general x8, matrix products, mm(): return jnp.dot(left, right, preferred_element_type=F32)  15.4 us
  transfers between devices with their start and end apart: 88, of which 41 were waited for; matrix products, arithmetic and copies ran while one was open for 39% of the time, Pallas kernels for 0%

profile of v1, /device:TPU:0, one launch (start us, length us, event | category | flops | bytes accessed | tf_op | source)
XLA Modules:
  0.0 363.6 jit_solution(14057346408426053304)
XLA Ops:
  1.9 5.1 %collective-permute-start.2 = (bf16[64,768]{1,0:T(8,128)(2,1)S(1)}, bf16[64,768]{1,0:T(8,128)(2,1)S(1)}, u32[]{:S(2)}, u32[]{:S(2)}) collective-permute-start(bf16[64,768]{1,0:T(8,128)(2,1)S(1)} %get-tuple-element.105), channel_id=1, source_target_pairs={{0,3},{1,0},{2,1},{3,2},{4,7},{5,4},{6,5},{7,6},{8,11},{9,8},{10,9... | collective-permute-start | bytes 294920 | tf_op jit(solution)/shard_map/ppermute | solution.py:139
  9.8 2.8 collective-permute-start.8
  13.8 16.6 %all_gather.3 = bf16[256,256]{1,0:T(8,128)(2,1)S(1)} all-gather(bf16[64,256]{1,0:T(8,128)(2,1)S(1)} %bitcast.507), channel_id=1, replica_groups=mesh['rows'=8,'kc'=4] {'kc'}, dimensions={0}, use_global_device_ids=true | all-gather | bytes 163840 | tf_op jit(solution)/shard_map/all_gather | solution.py:160
  37.2 2.5 convolution_convert_fusion.7
  43.9 2.9 fusion.135
  46.8 2.5 convolution_convert_fusion.4
  53.9 5.1 %fusion.7 = (bf16[256,3072]{1,0:T(8,128)(2,1)}, bf16[256,3072]{1,0:T(8,128)(2,1)}) fusion(f32[256,3072]{1,0:T(8,128)S(1)} %fusion.137, bf16[256,768]{1,0:T(8,128)(2,1)S(1)} %multiply_convert_fusion.3, bf16[768,3072]{1,0:T(8,128)(2,1)S(1)} %bitcast.509), kind=kOutput, calls=%fused_computation.11 | convolution fusion | flops 1225261056 | bytes 11403264 | tf_op jit(solution)/shard_map/dot_general | solution.py:27
  59.0 3.6 multiply_reduce_fusion.2
  66.5 2.9 multiply_reduce_fusion
  74.2 2.5 reshape.337
  76.8 2.7 fusion.138
  80.4 4.9 %fusion.18 = bf16[256,768]{1,0:T(8,128)(2,1)} fusion(f32[256,768]{1,0:T(8,128)S(1)} %get-tuple-element.142, bf16[256,3072]{1,0:T(8,128)(2,1)} %get-tuple-element.24, bf16[3072,768]{1,0:T(8,128)(2,1)} %param.18), kind=kOutput, calls=%fused_computation.38 | convolution fusion | flops 1208352768 | bytes 7471104 | tf_op jit(solution)/shard_map/dot_general | solution.py:27
  85.4 4.0 %reshape.331 = bf16[256,4,2,384]{3,2,1,0:T(2,128)(2,1)S(1)} reshape(bf16[256,3072]{1,0:T(8,128)(2,1)} %get-tuple-element.24) | data formatting | bytes 3145728 | tf_op jit(solution)/shard_map/reshape | solution.py:194
  99.2 2.5 fusion.139
  107.6 2.4 multiply_reduce_fusion.3
  111.1 3.8 %collective-permute-start.11 = (bf16[64,768]{1,0:T(8,128)(2,1)}, bf16[64,768]{1,0:T(8,128)(2,1)}, u32[]{:S(2)}, u32[]{:S(2)}) collective-permute-start(bf16[64,768]{1,0:T(8,128)(2,1)} %get-tuple-element.80), channel_id=1, source_target_pairs={{1,0},{2,1},{3,2},{0,3},{5,4},{6,5},{7,6},{4,7},{9,8},{10,9},{11,1... | collective-permute-start | bytes 294920 | tf_op jit(solution)/shard_map/ppermute | solution.py:150
  116.2 3.3 collective-permute-start.5
  120.3 4.4 %fusion.143 = f32[384,3072]{1,0:T(8,128)} fusion(bf16[256,384]{0,1:T(8,128)(2,1)S(1)} %bitcast.485, bf16[256,3072]{1,0:T(8,128)(2,1)} %get-tuple-element.23), kind=kOutput, calls=%fused_computation.406 | convolution fusion | flops 603979776 | bytes 6488064 | tf_op jit(solution)/shard_map/ta,tb->ab/dot_general | solution.py:35
  124.6 5.0 %constant_dynamic-slice_fusion.9 = (bf16[256,4,1,384]{3,2,1,0:T(2,128)(2,1)}, bf16[256,4,1,384]{3,2,1,0:T(2,128)(2,1)}) fusion(bf16[256,4,2,384]{3,2,1,0:T(2,128)(2,1)S(1)} %reshape.331, s32[]{:T(128)S(6)} %select_n.491, s32[]{:T(128)S(6)} %select_n.490), kind=kLoop, calls=%fused_computation.253 | loop fusion | bytes 3145736 | tf_op jit(solution)/shard_map/jit(dynamic_index_in_dim)/dynamic_slice | solution.py:196
  129.6 3.4 copy.137
  133.1 2.9 fusion.144
  137.3 2.5 fusion.142
  141.7 3.2 copy.138
  147.9 5.6 %collective-permute-done.4 = bf16[64,768]{1,0:T(8,128)(2,1)S(1)} collective-permute-done((bf16[64,768]{1,0:T(8,128)(2,1)S(1)}, bf16[64,768]{1,0:T(8,128)(2,1)S(1)}, u32[]{:S(2)}, u32[]{:S(2)}) %collective-permute-start.4) | collective-permute-done | bytes 98336 | tf_op jit(solution)/shard_map/ppermute | solution.py:150
  156.2 2.8 collective-permute-done.83
  172.0 2.4 fusion.14
  180.3 2.4 reshape.352
  202.1 2.5 collective-permute-start.53
  225.6 3.7 %collective-permute-start.18 = (bf16[48,192]{1,0:T(8,128)(2,1)S(1)}, bf16[48,192]{1,0:T(8,128)(2,1)S(1)}, u32[]{:S(2)}, u32[]{:S(2)}) collective-permute-start(bf16[48,192]{1,0:T(8,128)(2,1)S(1)} %get-tuple-element.132), channel_id=1, source_target_pairs={{0,3},{1,0},{2,1},{3,2},{4,7},{5,4},{6,5},{7,6},{8,11},{9,8},{10,9... | collective-permute-start | bytes 55304 | tf_op jit(solution)/shard_map/ppermute | solution.py:54
  230.8 4.1 %collective-permute-start.34 = (bf16[48,192]{1,0:T(8,128)(2,1)S(1)}, bf16[48,192]{1,0:T(8,128)(2,1)S(1)}, u32[]{:S(2)}, u32[]{:S(2)}) collective-permute-start(bf16[48,192]{1,0:T(8,128)(2,1)S(1)} %get-tuple-element.129), channel_id=1, source_target_pairs={{0,3},{1,0},{2,1},{3,2},{4,7},{5,4},{6,5},{7,6},{8,11},{9,8},{10,9... | collective-permute-start | bytes 55304 | tf_op jit(solution)/shard_map/ppermute | solution.py:54
  236.4 4.1 %collective-permute-start.29 = (bf16[48,192]{1,0:T(8,128)(2,1)S(1)}, bf16[48,192]{1,0:T(8,128)(2,1)S(1)}, u32[]{:S(2)}, u32[]{:S(2)}) collective-permute-start(bf16[48,192]{1,0:T(8,128)(2,1)S(1)} %get-tuple-element.126), channel_id=1, source_target_pairs={{0,3},{1,0},{2,1},{3,2},{4,7},{5,4},{6,5},{7,6},{8,11},{9,8},{10,9... | collective-permute-start | bytes 55304 | tf_op jit(solution)/shard_map/ppermute | solution.py:54
  242.0 4.2 %collective-permute-start.45 = (bf16[48,192]{1,0:T(8,128)(2,1)S(1)}, bf16[48,192]{1,0:T(8,128)(2,1)S(1)}, u32[]{:S(2)}, u32[]{:S(2)}) collective-permute-start(bf16[48,192]{1,0:T(8,128)(2,1)S(1)} %get-tuple-element.123), channel_id=1, source_target_pairs={{0,3},{1,0},{2,1},{3,2},{4,7},{5,4},{6,5},{7,6},{8,11},{9,8},{10,9... | collective-permute-start | bytes 55304 | tf_op jit(solution)/shard_map/ppermute | solution.py:54
  247.8 4.2 %collective-permute-start.40 = (bf16[48,192]{1,0:T(8,128)(2,1)S(1)}, bf16[48,192]{1,0:T(8,128)(2,1)S(1)}, u32[]{:S(2)}, u32[]{:S(2)}) collective-permute-start(bf16[48,192]{1,0:T(8,128)(2,1)S(1)} %get-tuple-element.120), channel_id=1, source_target_pairs={{0,3},{1,0},{2,1},{3,2},{4,7},{5,4},{6,5},{7,6},{8,11},{9,8},{10,9... | collective-permute-start | bytes 55304 | tf_op jit(solution)/shard_map/ppermute | solution.py:54
  253.4 4.1 %collective-permute-start.57 = (bf16[48,192]{1,0:T(8,128)(2,1)S(1)}, bf16[48,192]{1,0:T(8,128)(2,1)S(1)}, u32[]{:S(2)}, u32[]{:S(2)}) collective-permute-start(bf16[48,192]{1,0:T(8,128)(2,1)S(1)} %get-tuple-element.117), channel_id=1, source_target_pairs={{0,3},{1,0},{2,1},{3,2},{4,7},{5,4},{6,5},{7,6},{8,11},{9,8},{10,9... | collective-permute-start | bytes 55304 | tf_op jit(solution)/shard_map/ppermute | solution.py:54
  259.1 4.1 %collective-permute-start.52 = (bf16[48,192]{1,0:T(8,128)(2,1)S(1)}, bf16[48,192]{1,0:T(8,128)(2,1)S(1)}, u32[]{:S(2)}, u32[]{:S(2)}) collective-permute-start(bf16[48,192]{1,0:T(8,128)(2,1)S(1)} %get-tuple-element.114), channel_id=1, source_target_pairs={{0,3},{1,0},{2,1},{3,2},{4,7},{5,4},{6,5},{7,6},{8,11},{9,8},{10,9... | collective-permute-start | bytes 55304 | tf_op jit(solution)/shard_map/ppermute | solution.py:54
  264.7 3.2 collective-permute-done.51
  272.0 2.5 copy.96
  274.5 4.9 %reshape.373 = bf16[2,2,384,4,192]{2,1,0,4,3:T(2,128)(2,1)S(1)} reshape(bf16[1536,768]{0,1:T(8,128)(2,1)} %copy.96) | data formatting | bytes 4718592 | tf_op jit(solution)/shard_map/convert.39
  279.4 3.3 fusion.128
  286.5 3.2 constant_dynamic-slice_fusion.8
  292.0 9.3 %collective-permute-done.77 = bf16[2,192,4,192]{1,0,3,2:T(2,128)(2,1)S(1)} collective-permute-done((bf16[2,192,4,192]{1,0,3,2:T(2,128)(2,1)S(1)}, bf16[2,192,4,192]{1,0,3,2:T(2,128)(2,1)S(1)}, u32[]{:S(2)}, u32[]{:S(2)}) %collective-permute-start.77) | collective-permute-done | bytes 589856 | tf_op jit(solution)/shard_map/ppermute | solution.py:65
  302.1 2.4 constant_dynamic-slice_fusion.6
  305.7 2.7 collective-permute-done.72
  310.0 3.8 %add_convert_fusion.1 = bf16[384,3072]{1,0:T(8,128)(2,1)} fusion(f32[384,3072]{1,0:T(8,128)S(1)} %bitcast.458, bf16[256,384]{0,1:T(8,128)(2,1)} %collective-permute-done.58, bf16[256,3072]{1,0:T(8,128)(2,1)} %collective-permute-done.59), kind=kOutput, calls=%fused_computation.2 | convolution fusion | flops 606339072 | bytes 8847360 | tf_op jit(solution)/shard_map/ta,tb->ab/dot_general | solution.py:35
  313.8 4.8 %reshape.366 = bf16[2,2,96,4,768]{4,3,2,1,0:T(4,128)(2,1)S(1)} reshape(bf16[384,3072]{1,0:T(8,128)(2,1)} %add_convert_fusion.1) | data formatting | bytes 4718592 | tf_op jit(solution)/shard_map/convert.41
  330.8 3.8 %collective-permute-done.80 = bf16[192,192]{0,1:T(8,128)(2,1)S(1)} collective-permute-done((bf16[192,192]{0,1:T(8,128)(2,1)S(1)}, bf16[192,192]{0,1:T(8,128)(2,1)S(1)}, u32[]{:S(2)}, u32[]{:S(2)}) %collective-permute-start.80) | collective-permute-done | bytes 73760 | tf_op jit(solution)/shard_map/ppermute | solution.py:54
  336.6 4.5 %collective-permute-done.75 = bf16[192,192]{0,1:T(8,128)(2,1)S(1)} collective-permute-done((bf16[192,192]{0,1:T(8,128)(2,1)S(1)}, bf16[192,192]{0,1:T(8,128)(2,1)S(1)}, u32[]{:S(2)}, u32[]{:S(2)}) %collective-permute-start.75) | collective-permute-done | bytes 73760 | tf_op jit(solution)/shard_map/ppermute | solution.py:54
  344.7 4.3 %collective-permute-done.66 = bf16[48,4,768]{2,0,1:T(8,128)(2,1)S(1)} collective-permute-done((bf16[48,4,768]{2,0,1:T(8,128)(2,1)S(1)}, bf16[48,4,768]{2,0,1:T(8,128)(2,1)S(1)}, u32[]{:S(2)}, u32[]{:S(2)}) %collective-permute-start.66) | collective-permute-done | bytes 294944 | tf_op jit(solution)/shard_map/ppermute | solution.py:65
  (498 shorter events, 172.3 us)
Async XLA Ops:
  1.9 29.8 %collective-permute-start.2 = (bf16[64,768]{1,0:T(8,128)(2,1)S(1)}, bf16[64,768]{1,0:T(8,128)(2,1)S(1)}, u32[]{:S(2)}, u32[]{:S(2)}) collective-permute-start(bf16[64,768]{1,0:T(8,128)(2,1)S(1)} %get-tuple-element.105), channel_id=1, source_target_pairs={{0,3},{1,0},{2,1},{3,2},{4,7},{5,4},{6,5},{7,6},{8,11},{9,8},{10,9... | collective-permute-start | bytes 294920 | tf_op jit(solution)/shard_map/ppermute | solution.py:139
  7.0 24.8 %collective-permute-start.1 = (bf16[64,768]{1,0:T(8,128)(2,1)S(1)}, bf16[64,768]{1,0:T(8,128)(2,1)S(1)}, u32[]{:S(2)}, u32[]{:S(2)}) collective-permute-start(bf16[64,768]{1,0:T(8,128)(2,1)S(1)} %get-tuple-element.106), channel_id=1, source_target_pairs={{0,2},{1,3},{2,0},{3,1},{4,6},{5,7},{6,4},{7,5},{8,10},{9,11},{10,... | collective-permute-start | bytes 294920 | tf_op jit(solution)/shard_map/ppermute | solution.py:139
  7.0 24.8 %collective-permute-start = (bf16[64,768]{1,0:T(8,128)(2,1)S(1)}, bf16[64,768]{1,0:T(8,128)(2,1)S(1)}, u32[]{:S(2)}, u32[]{:S(2)}) collective-permute-start(bf16[64,768]{1,0:T(8,128)(2,1)S(1)} %get-tuple-element.104), channel_id=1, source_target_pairs={{0,1},{1,2},{2,3},{3,0},{4,5},{5,6},{6,7},{7,4},{8,9},{9,10},{10,1... | collective-permute-start | bytes 294920 | tf_op jit(solution)/shard_map/ppermute | solution.py:139
  9.8 40.4 %collective-permute-start.8 = (bf16[64,768]{1,0:T(8,128)(2,1)}, bf16[64,768]{1,0:T(8,128)(2,1)}, u32[]{:S(2)}, u32[]{:S(2)}) collective-permute-start(bf16[64,768]{1,0:T(8,128)(2,1)} %get-tuple-element.89), channel_id=1, source_target_pairs={{0,3},{1,0},{2,1},{3,2},{4,7},{5,4},{6,5},{7,6},{8,11},{9,8},{10,9... | collective-permute-start | bytes 294920 | tf_op jit(solution)/shard_map/ppermute | solution.py:139
  12.6 37.6 %collective-permute-start.7 = (bf16[64,768]{1,0:T(8,128)(2,1)}, bf16[64,768]{1,0:T(8,128)(2,1)}, u32[]{:S(2)}, u32[]{:S(2)}) collective-permute-start(bf16[64,768]{1,0:T(8,128)(2,1)} %get-tuple-element.90), channel_id=1, source_target_pairs={{0,2},{1,3},{2,0},{3,1},{4,6},{5,7},{6,4},{7,5},{8,10},{9,11},{10,... | collective-permute-start | bytes 294920 | tf_op jit(solution)/shard_map/ppermute | solution.py:139
  31.7 18.5 %collective-permute-start.6 = (bf16[64,768]{1,0:T(8,128)(2,1)}, bf16[64,768]{1,0:T(8,128)(2,1)}, u32[]{:S(2)}, u32[]{:S(2)}) collective-permute-start(bf16[64,768]{1,0:T(8,128)(2,1)} %get-tuple-element.88), channel_id=1, source_target_pairs={{0,1},{1,2},{2,3},{3,0},{4,5},{5,6},{6,7},{7,4},{8,9},{9,10},{10,1... | collective-permute-start | bytes 294920 | tf_op jit(solution)/shard_map/ppermute | solution.py:139
  79.5 91.8 %collective-permute-start.13 = (bf16[256,768]{0,1:T(8,128)(2,1)S(1)}, bf16[256,768]{0,1:T(8,128)(2,1)}, u32[]{:S(2)}, u32[]{:S(2)}) collective-permute-start(bf16[256,768]{0,1:T(8,128)(2,1)S(1)} %bitcast.467), channel_id=1, source_target_pairs={{0,4},{4,0},{8,12},{12,8},{16,20},{20,16},{24,28},{28,24},{1,5},{5... | collective-permute-start | bytes 1179656 | tf_op jit(solution)/shard_map/ppermute | solution.py:65
  111.1 33.8 %collective-permute-start.11 = (bf16[64,768]{1,0:T(8,128)(2,1)}, bf16[64,768]{1,0:T(8,128)(2,1)}, u32[]{:S(2)}, u32[]{:S(2)}) collective-permute-start(bf16[64,768]{1,0:T(8,128)(2,1)} %get-tuple-element.80), channel_id=1, source_target_pairs={{1,0},{2,1},{3,2},{0,3},{5,4},{6,5},{7,6},{4,7},{9,8},{10,9},{11,1... | collective-permute-start | bytes 294920 | tf_op jit(solution)/shard_map/ppermute | solution.py:150
  114.9 31.1 %collective-permute-start.10 = (bf16[64,768]{1,0:T(8,128)(2,1)}, bf16[64,768]{1,0:T(8,128)(2,1)}, u32[]{:S(2)}, u32[]{:S(2)}) collective-permute-start(bf16[64,768]{1,0:T(8,128)(2,1)} %get-tuple-element.81), channel_id=1, source_target_pairs={{2,0},{3,1},{0,2},{1,3},{6,4},{7,5},{4,6},{5,7},{10,8},{11,9},{8,1... | collective-permute-start | bytes 294920 | tf_op jit(solution)/shard_map/ppermute | solution.py:150
  114.9 31.3 %collective-permute-start.9 = (bf16[64,768]{1,0:T(8,128)(2,1)}, bf16[64,768]{1,0:T(8,128)(2,1)}, u32[]{:S(2)}, u32[]{:S(2)}) collective-permute-start(bf16[64,768]{1,0:T(8,128)(2,1)} %get-tuple-element.82), channel_id=1, source_target_pairs={{3,0},{0,1},{1,2},{2,3},{7,4},{4,5},{5,6},{6,7},{11,8},{8,9},{9,10... | collective-permute-start | bytes 294920 | tf_op jit(solution)/shard_map/ppermute | solution.py:150
  116.2 31.1 %collective-permute-start.5 = (bf16[64,768]{1,0:T(8,128)(2,1)}, bf16[64,768]{1,0:T(8,128)(2,1)}, u32[]{:S(2)}, u32[]{:S(2)}) collective-permute-start(bf16[64,768]{1,0:T(8,128)(2,1)} %get-tuple-element.96), channel_id=1, source_target_pairs={{1,0},{2,1},{3,2},{0,3},{5,4},{6,5},{7,6},{4,7},{9,8},{10,9},{11,1... | collective-permute-start | bytes 294920 | tf_op jit(solution)/shard_map/ppermute | solution.py:150
  144.9 8.6 %collective-permute-start.4 = (bf16[64,768]{1,0:T(8,128)(2,1)S(1)}, bf16[64,768]{1,0:T(8,128)(2,1)S(1)}, u32[]{:S(2)}, u32[]{:S(2)}) collective-permute-start(bf16[64,768]{1,0:T(8,128)(2,1)S(1)} %copy-done.59), channel_id=1, source_target_pairs={{2,0},{3,1},{0,2},{1,3},{6,4},{7,5},{4,6},{5,7},{10,8},{11,9},{8,1... | collective-permute-start | bytes 294920 | tf_op jit(solution)/shard_map/ppermute | solution.py:150
  146.0 7.5 %collective-permute-start.3 = (bf16[64,768]{1,0:T(8,128)(2,1)S(1)}, bf16[64,768]{1,0:T(8,128)(2,1)S(1)}, u32[]{:S(2)}, u32[]{:S(2)}) collective-permute-start(bf16[64,768]{1,0:T(8,128)(2,1)S(1)} %copy-done.58), channel_id=1, source_target_pairs={{3,0},{0,1},{1,2},{2,3},{7,4},{4,5},{5,6},{6,7},{11,8},{8,9},{9,10... | collective-permute-start | bytes 294920 | tf_op jit(solution)/shard_map/ppermute | solution.py:150
  146.2 8.2 %collective-permute-start.82 = (f32[2,2,4,2240]{3,2,1,0:T(4,128)S(1)}, f32[2,2,4,2240]{3,2,1,0:T(4,128)S(1)}, u32[]{:S(2)}, u32[]{:S(2)}) collective-permute-start(f32[2,2,4,2240]{3,2,1,0:T(4,128)S(1)} %fusion.54), channel_id=1, source_target_pairs={{0,4},{4,0},{8,12},{12,8},{16,20},{20,16},{24,28},{28,24},{1,5},{5... | collective-permute-start | bytes 430088 | tf_op jit(solution)/shard_map/ppermute | solution.py:65
  147.3 29.3 %collective-permute-start.35 = (bf16[256,768]{1,0:T(8,128)(2,1)}, bf16[256,768]{1,0:T(8,128)(2,1)}, u32[]{:S(2)}, u32[]{:S(2)}) collective-permute-start(bf16[256,768]{1,0:T(8,128)(2,1)} %convolution_convert_fusion), channel_id=1, source_target_pairs={{0,4},{4,0},{8,12},{12,8},{16,20},{20,16},{24,28},{28,24},{1,5},{5... | collective-permute-start | bytes 1179656 | tf_op jit(solution)/shard_map/ppermute | solution.py:65
  166.9 16.9 %collective-permute-start.24 = (bf16[256,768]{1,0:T(8,128)(2,1)S(1)}, bf16[256,768]{1,0:T(8,128)(2,1)}, u32[]{:S(2)}, u32[]{:S(2)}) collective-permute-start(bf16[256,768]{1,0:T(8,128)(2,1)S(1)} %copy-done.20), channel_id=1, source_target_pairs={{0,4},{4,0},{8,12},{12,8},{16,20},{20,16},{24,28},{28,24},{1,5},{5... | collective-permute-start | bytes 1179656 | tf_op jit(solution)/shard_map/ppermute | solution.py:65
  168.3 23.4 %collective-permute-start.47 = (bf16[256,768]{1,0:T(8,128)(2,1)}, bf16[256,768]{1,0:T(8,128)(2,1)}, u32[]{:S(2)}, u32[]{:S(2)}) collective-permute-start(bf16[256,768]{1,0:T(8,128)(2,1)} %get-tuple-element.21), channel_id=1, source_target_pairs={{0,4},{4,0},{8,12},{12,8},{16,20},{20,16},{24,28},{28,24},{1,5},{5... | collective-permute-start | bytes 1179656 | tf_op jit(solution)/shard_map/ppermute | solution.py:65
  171.1 98.8 %collective-permute-start.71 = (bf16[256,768]{1,0:T(8,128)(2,1)S(1)}, bf16[256,768]{1,0:T(8,128)(2,1)}, u32[]{:S(2)}, u32[]{:S(2)}) collective-permute-start(bf16[256,768]{1,0:T(8,128)(2,1)S(1)} %bitcast.462), channel_id=1, source_target_pairs={{0,4},{4,0},{8,12},{12,8},{16,20},{20,16},{24,28},{28,24},{1,5},{5... | collective-permute-start | bytes 1179656 | tf_op jit(solution)/shard_map/ppermute | solution.py:65
  171.8 18.4 %collective-permute-start.46 = (bf16[256,384]{0,1:T(8,128)(2,1)}, bf16[256,384]{0,1:T(8,128)(2,1)}, u32[]{:S(2)}, u32[]{:S(2)}) collective-permute-start(bf16[256,384]{0,1:T(8,128)(2,1)} %bitcast.501), channel_id=1, source_target_pairs={{0,4},{4,0},{8,12},{12,8},{16,20},{20,16},{24,28},{28,24},{1,5},{5... | collective-permute-start | bytes 589832 | tf_op jit(solution)/shard_map/ppermute | solution.py:65
  176.6 93.4 %collective-permute-start.70 = (bf16[256,1536]{0,1:T(8,128)(2,1)}, bf16[256,1536]{0,1:T(8,128)(2,1)}, u32[]{:S(2)}, u32[]{:S(2)}) collective-permute-start(bf16[256,1536]{0,1:T(8,128)(2,1)} %bitcast.486), channel_id=1, source_target_pairs={{0,4},{4,0},{8,12},{12,8},{16,20},{20,16},{24,28},{28,24},{1,5},{5... | collective-permute-start | bytes 2359304 | tf_op jit(solution)/shard_map/ppermute | solution.py:65
  183.8 11.6 %collective-permute-start.19 = (bf16[2,48,4,192]{3,1,2,0:T(8,128)(2,1)}, bf16[2,48,4,192]{3,1,2,0:T(8,128)(2,1)}, u32[]{:S(2)}, u32[]{:S(2)}) collective-permute-start(bf16[2,48,4,192]{3,1,2,0:T(8,128)(2,1)} %bitcast.453), channel_id=1, source_target_pairs={{0,16},{4,20},{8,24},{12,28},{16,0},{20,4},{24,8},{28,12},{1,17},{... | collective-permute-start | bytes 442376 | tf_op jit(solution)/shard_map/ppermute | solution.py:65
  190.2 7.0 %collective-permute-start.14 = (bf16[2,48,4,192]{3,1,2,0:T(8,128)(2,1)}, bf16[2,48,4,192]{3,1,2,0:T(8,128)(2,1)}, u32[]{:S(2)}, u32[]{:S(2)}) collective-permute-start(bf16[2,48,4,192]{3,1,2,0:T(8,128)(2,1)} %bitcast.454), channel_id=1, source_target_pairs={{0,8},{4,12},{8,0},{12,4},{16,24},{20,28},{24,16},{28,20},{1,9},{5... | collective-permute-start | bytes 442376 | tf_op jit(solution)/shard_map/ppermute | solution.py:65
  191.7 7.9 %collective-permute-start.30 = (bf16[2,48,4,192]{3,1,2,0:T(8,128)(2,1)}, bf16[2,48,4,192]{3,1,2,0:T(8,128)(2,1)}, u32[]{:S(2)}, u32[]{:S(2)}) collective-permute-start(bf16[2,48,4,192]{3,1,2,0:T(8,128)(2,1)} %bitcast.451), channel_id=1, source_target_pairs={{0,16},{4,20},{8,24},{12,28},{16,0},{20,4},{24,8},{28,12},{1,17},{... | collective-permute-start | bytes 442376 | tf_op jit(solution)/shard_map/ppermute | solution.py:65
  195.4 6.7 %collective-permute-start.25 = (bf16[2,48,4,192]{3,1,2,0:T(8,128)(2,1)S(1)}, bf16[2,48,4,192]{3,1,2,0:T(8,128)(2,1)S(1)}, u32[]{:S(2)}, u32[]{:S(2)}) collective-permute-start(bf16[2,48,4,192]{3,1,2,0:T(8,128)(2,1)S(1)} %bitcast.500), channel_id=1, source_target_pairs={{0,8},{4,12},{8,0},{12,4},{16,24},{20,28},{24,16},{28,20},{1,9},{5... | collective-permute-start | bytes 442376 | tf_op jit(solution)/shard_map/ppermute | solution.py:65
  197.2 7.4 %collective-permute-start.41 = (bf16[2,48,4,192]{3,1,2,0:T(8,128)(2,1)S(1)}, bf16[2,48,4,192]{3,1,2,0:T(8,128)(2,1)S(1)}, u32[]{:S(2)}, u32[]{:S(2)}) collective-permute-start(bf16[2,48,4,192]{3,1,2,0:T(8,128)(2,1)S(1)} %bitcast.499), channel_id=1, source_target_pairs={{0,16},{4,20},{8,24},{12,28},{16,0},{20,4},{24,8},{28,12},{1,17},{... | collective-permute-start | bytes 442376 | tf_op jit(solution)/shard_map/ppermute | solution.py:65
  199.6 7.9 %collective-permute-start.36 = (bf16[2,48,4,192]{3,1,2,0:T(8,128)(2,1)S(1)}, bf16[2,48,4,192]{3,1,2,0:T(8,128)(2,1)S(1)}, u32[]{:S(2)}, u32[]{:S(2)}) collective-permute-start(bf16[2,48,4,192]{3,1,2,0:T(8,128)(2,1)S(1)} %bitcast.498), channel_id=1, source_target_pairs={{0,8},{4,12},{8,0},{12,4},{16,24},{20,28},{24,16},{28,20},{1,9},{5... | collective-permute-start | bytes 442376 | tf_op jit(solution)/shard_map/ppermute | solution.py:65
  202.1 6.9 %collective-permute-start.53 = (bf16[2,48,4,192]{3,1,2,0:T(8,128)(2,1)S(1)}, bf16[2,48,4,192]{3,1,2,0:T(8,128)(2,1)S(1)}, u32[]{:S(2)}, u32[]{:S(2)}) collective-permute-start(bf16[2,48,4,192]{3,1,2,0:T(8,128)(2,1)S(1)} %bitcast.497), channel_id=1, source_target_pairs={{0,16},{4,20},{8,24},{12,28},{16,0},{20,4},{24,8},{28,12},{1,17},{... | collective-permute-start | bytes 442376 | tf_op jit(solution)/shard_map/ppermute | solution.py:65
  204.7 6.8 %collective-permute-start.48 = (bf16[2,48,4,192]{3,1,2,0:T(8,128)(2,1)S(1)}, bf16[2,48,4,192]{3,1,2,0:T(8,128)(2,1)S(1)}, u32[]{:S(2)}, u32[]{:S(2)}) collective-permute-start(bf16[2,48,4,192]{3,1,2,0:T(8,128)(2,1)S(1)} %bitcast.496), channel_id=1, source_target_pairs={{0,8},{4,12},{8,0},{12,4},{16,24},{20,28},{24,16},{28,20},{1,9},{5... | collective-permute-start | bytes 442376 | tf_op jit(solution)/shard_map/ppermute | solution.py:65
  217.8 5.9 %collective-permute-start.54 = (bf16[48,4,192]{2,0,1:T(8,128)(2,1)S(1)}, bf16[48,4,192]{2,0,1:T(8,128)(2,1)S(1)}, u32[]{:S(2)}, u32[]{:S(2)}) collective-permute-start(bf16[48,4,192]{2,0,1:T(8,128)(2,1)S(1)} %dynamic-slice_bitcast_fusion.10), channel_id=1, source_target_pairs={{0,8},{4,12},{8,0},{12,4},{16,24},{20,28},{24,16},{28,20},{1,9},{5... | collective-permute-start | bytes 221192 | tf_op jit(solution)/shard_map/ppermute | solution.py:65
  264.7 45.3 %collective-permute-start.59 = (bf16[256,3072]{1,0:T(8,128)(2,1)}, bf16[256,3072]{1,0:T(8,128)(2,1)}, u32[]{:S(2)}, u32[]{:S(2)}) collective-permute-start(bf16[256,3072]{1,0:T(8,128)(2,1)} %get-tuple-element.23), channel_id=1, source_target_pairs={{0,4},{4,0},{8,12},{12,8},{16,20},{20,16},{24,28},{28,24},{1,5},{5... | collective-permute-start | bytes 4718600 | tf_op jit(solution)/shard_map/ppermute | solution.py:65
  267.9 42.0 %collective-permute-start.58 = (bf16[256,384]{0,1:T(8,128)(2,1)}, bf16[256,384]{0,1:T(8,128)(2,1)}, u32[]{:S(2)}, u32[]{:S(2)}) collective-permute-start(bf16[256,384]{0,1:T(8,128)(2,1)} %bitcast.115), channel_id=1, source_target_pairs={{0,4},{4,0},{8,12},{12,8},{16,20},{20,16},{24,28},{28,24},{1,5},{5... | collective-permute-start | bytes 589832 | tf_op jit(solution)/shard_map/ppermute | solution.py:65
  283.3 18.0 %collective-permute-start.77 = (bf16[2,192,4,192]{1,0,3,2:T(2,128)(2,1)S(1)}, bf16[2,192,4,192]{1,0,3,2:T(2,128)(2,1)S(1)}, u32[]{:S(2)}, u32[]{:S(2)}) collective-permute-start(bf16[2,192,4,192]{1,0,3,2:T(2,128)(2,1)S(1)} %dynamic-slice_bitcast_fusion), channel_id=1, source_target_pairs={{0,16},{4,20},{8,24},{12,28},{16,0},{20,4},{24,8},{28,12},{1,17},{... | collective-permute-start | bytes 1769480 | tf_op jit(solution)/shard_map/ppermute | solution.py:65
  289.9 18.6 %collective-permute-start.72 = (bf16[2,192,4,192]{1,3,2,0:T(8,128)(2,1)S(1)}, bf16[2,192,4,192]{1,3,2,0:T(8,128)(2,1)S(1)}, u32[]{:S(2)}, u32[]{:S(2)}) collective-permute-start(bf16[2,192,4,192]{1,3,2,0:T(8,128)(2,1)S(1)} %bitcast.487), channel_id=1, source_target_pairs={{0,8},{4,12},{8,0},{12,4},{16,24},{20,28},{24,16},{28,20},{1,9},{5... | collective-permute-start | bytes 1769480 | tf_op jit(solution)/shard_map/ppermute | solution.py:65
  305.3 17.8 %collective-permute-start.78 = (bf16[192,4,192]{0,2,1:T(8,128)(2,1)}, bf16[192,4,192]{0,2,1:T(8,128)(2,1)}, u32[]{:S(2)}, u32[]{:S(2)}) collective-permute-start(bf16[192,4,192]{0,2,1:T(8,128)(2,1)} %bitcast.446), channel_id=1, source_target_pairs={{0,8},{4,12},{8,0},{12,4},{16,24},{20,28},{24,16},{28,20},{1,9},{5... | collective-permute-start | bytes 884744 | tf_op jit(solution)/shard_map/ppermute | solution.py:65
  309.5 14.9 %collective-permute-start.73 = (bf16[192,4,192]{0,2,1:T(8,128)(2,1)}, bf16[192,4,192]{0,2,1:T(8,128)(2,1)}, u32[]{:S(2)}, u32[]{:S(2)}) collective-permute-start(bf16[192,4,192]{0,2,1:T(8,128)(2,1)} %dynamic-slice_bitcast_fusion.1), channel_id=1, source_target_pairs={{0,16},{4,20},{8,24},{12,28},{16,0},{20,4},{24,8},{28,12},{1,17},{... | collective-permute-start | bytes 884744 | tf_op jit(solution)/shard_map/ppermute | solution.py:65
  319.9 22.2 %collective-permute-start.65 = (bf16[2,48,4,768]{3,1,2,0:T(8,128)(2,1)S(1)}, bf16[2,48,4,768]{3,1,2,0:T(8,128)(2,1)S(1)}, u32[]{:S(2)}, u32[]{:S(2)}) collective-permute-start(bf16[2,48,4,768]{3,1,2,0:T(8,128)(2,1)S(1)} %bitcast.490), channel_id=1, source_target_pairs={{0,16},{4,20},{8,24},{12,28},{16,0},{20,4},{24,8},{28,12},{1,17},{... | collective-permute-start | bytes 1769480 | tf_op jit(solution)/shard_map/ppermute | solution.py:65
  322.0 21.4 %collective-permute-start.60 = (bf16[2,48,4,768]{3,1,2,0:T(8,128)(2,1)S(1)}, bf16[2,48,4,768]{3,1,2,0:T(8,128)(2,1)S(1)}, u32[]{:S(2)}, u32[]{:S(2)}) collective-permute-start(bf16[2,48,4,768]{3,1,2,0:T(8,128)(2,1)S(1)} %bitcast.489), channel_id=1, source_target_pairs={{0,8},{4,12},{8,0},{12,4},{16,24},{20,28},{24,16},{28,20},{1,9},{5... | collective-permute-start | bytes 1769480 | tf_op jit(solution)/shard_map/ppermute | solution.py:65
  324.3 10.3 %collective-permute-start.80 = (bf16[192,192]{0,1:T(8,128)(2,1)S(1)}, bf16[192,192]{0,1:T(8,128)(2,1)S(1)}, u32[]{:S(2)}, u32[]{:S(2)}) collective-permute-start(bf16[192,192]{0,1:T(8,128)(2,1)S(1)} %get-tuple-element.54), channel_id=1, source_target_pairs={{0,2},{1,3},{2,0},{3,1},{4,6},{5,7},{6,4},{7,5},{8,10},{9,11},{10,... | collective-permute-start | bytes 221192 | tf_op jit(solution)/shard_map/ppermute | solution.py:54
  324.4 10.2 %collective-permute-start.79 = (bf16[192,192]{0,1:T(8,128)(2,1)S(1)}, bf16[192,192]{0,1:T(8,128)(2,1)S(1)}, u32[]{:S(2)}, u32[]{:S(2)}) collective-permute-start(bf16[192,192]{0,1:T(8,128)(2,1)S(1)} %get-tuple-element.52), channel_id=1, source_target_pairs={{0,1},{1,2},{2,3},{3,0},{4,5},{5,6},{6,7},{7,4},{8,9},{9,10},{10,1... | collective-permute-start | bytes 221192 | tf_op jit(solution)/shard_map/ppermute | solution.py:54
  329.0 7.7 %collective-permute-start.76 = (bf16[192,192]{0,1:T(8,128)(2,1)S(1)}, bf16[192,192]{0,1:T(8,128)(2,1)S(1)}, u32[]{:S(2)}, u32[]{:S(2)}) collective-permute-start(bf16[192,192]{0,1:T(8,128)(2,1)S(1)} %get-tuple-element.50), channel_id=1, source_target_pairs={{0,3},{1,0},{2,1},{3,2},{4,7},{5,4},{6,5},{7,6},{8,11},{9,8},{10,9... | collective-permute-start | bytes 221192 | tf_op jit(solution)/shard_map/ppermute | solution.py:54
  334.6 6.6 %collective-permute-start.75 = (bf16[192,192]{0,1:T(8,128)(2,1)S(1)}, bf16[192,192]{0,1:T(8,128)(2,1)S(1)}, u32[]{:S(2)}, u32[]{:S(2)}) collective-permute-start(bf16[192,192]{0,1:T(8,128)(2,1)S(1)} %get-tuple-element.51), channel_id=1, source_target_pairs={{0,2},{1,3},{2,0},{3,1},{4,6},{5,7},{6,4},{7,5},{8,10},{9,11},{10,... | collective-permute-start | bytes 221192 | tf_op jit(solution)/shard_map/ppermute | solution.py:54
  334.6 6.6 %collective-permute-start.74 = (bf16[192,192]{0,1:T(8,128)(2,1)S(1)}, bf16[192,192]{0,1:T(8,128)(2,1)S(1)}, u32[]{:S(2)}, u32[]{:S(2)}) collective-permute-start(bf16[192,192]{0,1:T(8,128)(2,1)S(1)} %get-tuple-element.49), channel_id=1, source_target_pairs={{0,1},{1,2},{2,3},{3,0},{4,5},{5,6},{6,7},{7,4},{8,9},{9,10},{10,1... | collective-permute-start | bytes 221192 | tf_op jit(solution)/shard_map/ppermute | solution.py:54
  342.2 6.8 %collective-permute-start.66 = (bf16[48,4,768]{2,0,1:T(8,128)(2,1)S(1)}, bf16[48,4,768]{2,0,1:T(8,128)(2,1)S(1)}, u32[]{:S(2)}, u32[]{:S(2)}) collective-permute-start(bf16[48,4,768]{2,0,1:T(8,128)(2,1)S(1)} %dynamic-slice_bitcast_fusion.2), channel_id=1, source_target_pairs={{0,8},{4,12},{8,0},{12,4},{16,24},{20,28},{24,16},{28,20},{1,9},{5... | collective-permute-start | bytes 884744 | tf_op jit(solution)/shard_map/ppermute | solution.py:65
  343.6 9.3 %collective-permute-start.61 = (bf16[48,4,768]{2,0,1:T(8,128)(2,1)S(1)}, bf16[48,4,768]{2,0,1:T(8,128)(2,1)S(1)}, u32[]{:S(2)}, u32[]{:S(2)}) collective-permute-start(bf16[48,4,768]{2,0,1:T(8,128)(2,1)S(1)} %dynamic-slice_bitcast_fusion.3), channel_id=1, source_target_pairs={{0,16},{4,20},{8,24},{12,28},{16,0},{20,4},{24,8},{28,12},{1,17},{... | collective-permute-start | bytes 884744 | tf_op jit(solution)/shard_map/ppermute | solution.py:65
  349.1 7.1 %collective-permute-start.69 = (bf16[48,768]{1,0:T(8,128)(2,1)S(1)}, bf16[48,768]{1,0:T(8,128)(2,1)S(1)}, u32[]{:S(2)}, u32[]{:S(2)}) collective-permute-start(bf16[48,768]{1,0:T(8,128)(2,1)S(1)} %get-tuple-element.111), channel_id=1, source_target_pairs={{0,3},{1,0},{2,1},{3,2},{4,7},{5,4},{6,5},{7,6},{8,11},{9,8},{10,9... | collective-permute-start | bytes 221192 | tf_op jit(solution)/shard_map/ppermute | solution.py:54
  351.1 6.4 %collective-permute-start.68 = (bf16[48,768]{1,0:T(8,128)(2,1)S(1)}, bf16[48,768]{1,0:T(8,128)(2,1)S(1)}, u32[]{:S(2)}, u32[]{:S(2)}) collective-permute-start(bf16[48,768]{1,0:T(8,128)(2,1)S(1)} %get-tuple-element.112), channel_id=1, source_target_pairs={{0,2},{1,3},{2,0},{3,1},{4,6},{5,7},{6,4},{7,5},{8,10},{9,11},{10,... | collective-permute-start | bytes 221192 | tf_op jit(solution)/shard_map/ppermute | solution.py:54
  351.1 6.4 %collective-permute-start.67 = (bf16[48,768]{1,0:T(8,128)(2,1)S(1)}, bf16[48,768]{1,0:T(8,128)(2,1)S(1)}, u32[]{:S(2)}, u32[]{:S(2)}) collective-permute-start(bf16[48,768]{1,0:T(8,128)(2,1)S(1)} %get-tuple-element.110), channel_id=1, source_target_pairs={{0,1},{1,2},{2,3},{3,0},{4,5},{5,6},{6,7},{7,4},{8,9},{9,10},{10,1... | collective-permute-start | bytes 221192 | tf_op jit(solution)/shard_map/ppermute | solution.py:54
  356.3 6.2 %collective-permute-start.62 = (bf16[48,768]{1,0:T(8,128)(2,1)S(1)}, bf16[48,768]{1,0:T(8,128)(2,1)S(1)}, u32[]{:S(2)}, u32[]{:S(2)}) collective-permute-start(bf16[48,768]{1,0:T(8,128)(2,1)S(1)} %get-tuple-element.107), channel_id=1, source_target_pairs={{0,1},{1,2},{2,3},{3,0},{4,5},{5,6},{6,7},{7,4},{8,9},{9,10},{10,1... | collective-permute-start | bytes 221192 | tf_op jit(solution)/shard_map/ppermute | solution.py:54
  (119 other events, 738.8 us)

commit v2 on v1

--- a/solution.py
+++ b/solution.py
@@ -1,8 +1,11 @@
+import functools
 import math
 
 import jax
 import jax.numpy as jnp
 from jax import lax
+from jax.experimental import pallas as pl
+from jax.experimental.pallas import tpu as pltpu
 from jax.sharding import PartitionSpec as P
 
 HEAD = 64
@@ -94,7 +97,7 @@
     return jnp.concatenate(done, axis=0)
 
 
-def local(
+def general(
     inputs,
     w_query,
     w_key,
@@ -236,34 +239,569 @@
         d_e = lax.dynamic_update_slice(
             jnp.zeros((seq_len, d_e.shape[1]), F32), d_e, (my_part * mine, 0)
         )
-    e_rows, e_cols = seq_len // n_rows, d_e.shape[1] // n_kc
+    small = small_sum(grid, d_e, jnp.stack([gg_attn, gg_ffn]))
+    return (output, grad_in, *attn, g_up, g_down, *small)
+
+
+VMEM_LIMIT = 48 * 1024 * 1024
+MANY = pl.BlockSpec(memory_space=pl.ANY)
+SCALARS = pl.BlockSpec(memory_space=pltpu.SMEM)
+VM = pl.BlockSpec(memory_space=pltpu.VMEM)
+
+
+def here():
+    row = lax.axis_index("rows")
+    return row & 1, row >> 1, lax.axis_index("kc")
+
+
+def nt(left, right):
+    return lax.dot_general(left, right, (((1,), (1,)), ((), ())), preferred_element_type=F32)
+
+
+def sds(*shape, dtype=BF):
+    return jax.ShapeDtypeStruct(shape, dtype)
+
+
+def call(body, outs, args, specs=None, scratch=(), out_specs=None, cost=None):
+    return pl.pallas_call(
+        body,
+        out_shape=outs,
+        in_specs=specs or [VM] * len(args),
+        out_specs=out_specs or [VM] * len(outs),
+        scratch_shapes=list(scratch),
+        compiler_params=pltpu.CompilerParams(vmem_limit_bytes=VMEM_LIMIT),
+        cost_estimate=pl.CostEstimate(
+            flops=cost or 1000, bytes_accessed=1000000, transcendentals=0
+        ),
+    )(*args)
+
+
+def transposed(value):
+    return jnp.transpose(value.astype(F32)).astype(BF)
+
+
+def pack_kernel(n, x_ref, e_ref, c_ref, *outs):
+    _, _, z = here()
+    width = x_ref.shape[2]
+    e_t = transposed(e_ref[...])
+    for j in range(n):
+        outs[j][:, :width] = x_ref[(z + j) & (n - 1)]
+        outs[j][:, width:] = e_t
+        outs[n + j][...] = c_ref[(z + j) & (n - 1)]
+
+
+def gelu_both(u):
+    s = math.sqrt(2.0 / math.pi)
+    u2 = u * u
+    th = jnp.tanh(u * (s + (s * 0.044715) * u2))
+    half = 0.5 * (1.0 + th)
+    slope = half + (0.5 * u) * (1.0 - th * th) * (s + (3.0 * s * 0.044715) * u2)
+    return u * half, slope
+
+
+def halves(value):
+    low = lax.broadcasted_iota(jnp.int32, value.shape, 1) < HEAD
+    zero = jnp.zeros_like(value)
+    return jnp.where(low, value, zero), jnp.where(low, zero, value)
+
+
+def softmax_rows(scores):
+    expo = jnp.exp(scores - jnp.max(scores, axis=0, keepdims=True))
+    return expo / jnp.sum(expo, axis=0, keepdims=True)
+
+
+def forward_kernel(n, *refs):
+    xe = refs[:n]
+    len_ref, ga_ref, gf_ref = refs[n : n + 3]
+    w_hbm = refs[n + 3 : n + 8]
+    outs = refs[n + 8 : n + 21]
+    w_vm = refs[n + 21 : n + 26]
+    act_s, lt_s, gp_s, q_s, k_s, v_s, kc_s, vc_s, mid_s, x_s, em_s, et_s, att_t = refs[
+        n + 26 : n + 39
+    ]
+    w_sem, o_sem = refs[n + 39 :]
+    loads = [
+        pltpu.make_async_copy(a, b, w_sem.at[i]) for i, (a, b) in enumerate(zip(w_hbm, w_vm))
+    ]
+    for load in loads:
+        load.start()
+    core, xy, z = here()
+    t, wide = xe[0].shape
+    mine = t * n
+    width = x_s.shape[1]
+    ff = w_vm[4].shape[1]
+    stores = []
+
+    def store(src, i):
+        stores.append(pltpu.make_async_copy(src, outs[i], o_sem.at[i]))
+        stores[-1].start()
+
+    def rows_by_core(i, value):
+        value_t = jnp.transpose(value).astype(BF)
+        part = width // 8
+        for b in range(4):
+            for a in range(2):
+                first = (2 * b + a) * part
+                lt_s[a ^ core, i, b ^ xy] = value_t[first : first + part]
+
+    for j in range(n):
+        at = pl.multiple_of(((z - j) & (n - 1)) * t, t)
+        x_s[pl.ds(at, t), :] = xe[j][:, :width]
+        et_s[pl.ds(at, t), :] = xe[j][:, width:]
+    store(x_s, 11)
+    x = x_s[...].astype(F32)
+    n1, _ = normed(x)
+    h = n1 * ga_ref[...]
+    rows_by_core(0, h)
+    h = h.astype(BF)
+    keep = lax.broadcasted_iota(jnp.int32, et_s.shape, 1) < len_ref[z, 0]
+    e_t = jnp.where(keep, et_s[...].astype(F32), 0.0)
+    em_s[...] = jnp.transpose(e_t).astype(BF)
+    store(em_s, 12)
+    e_t = e_t.astype(BF)
+    loads[0].wait()
+    q_s[...] = mm(h, w_vm[0][...]).astype(BF)
+    store(q_s, 5)
+    loads[1].wait()
+    k_s[...] = mm(h, w_vm[1][...]).astype(BF)
+    store(k_s, 6)
+    loads[2].wait()
+    v_s[...] = mm(h, w_vm[2][...]).astype(BF)
+    store(v_s, 7)
+    kc_s[...] = mm(e_t, k_s[...]).astype(BF)
+    store(kc_s, 8)
+    v_comp = mm(e_t, v_s[...])
+    vc_s[...] = v_comp.astype(BF)
+    store(vc_s, 9)
+    vc_t = jnp.transpose(v_comp).astype(BF)
+    for p in range(width // 128):
+        lanes = slice(128 * p, 128 * p + 128)
+        q2 = q_s[:, lanes]
+        for i, kc in enumerate(halves(kc_s[:, lanes])):
+            probs = softmax_rows(nt(kc, q2) * HEAD ** (-0.5)).astype(BF)
+            first = 128 * p + HEAD * i
+            att_t[first : first + HEAD, :] = mm(vc_t[first : first + HEAD, :], probs)
+    att = jnp.transpose(att_t[...])
+    rows_by_core_t = att_t[...].astype(BF)
+    part = width // 8
+    for b in range(4):
+        for a in range(2):
+            first = (2 * b + a) * part
+            lt_s[a ^ core, 1, b ^ xy] = rows_by_core_t[first : first + part]
+    loads[3].wait()
+    mid = x + mm(att.astype(BF), w_vm[3][...])
+    mid_s[...] = mid
+    store(mid_s, 10)
+    n2, _ = normed(mid)
+    h2 = n2 * gf_ref[...]
+    rows_by_core(2, h2)
+    store(lt_s.at[0], 2)
+    store(lt_s.at[1], 3)
+    h2 = h2.astype(BF)
+    loads[4].wait()
+    step = ff // 4
+    for b in range(4):
+        act, slope = gelu_both(mm(h2, w_vm[4][:, b * step : (b + 1) * step]))
+        gp_s[:, b * step : (b + 1) * step] = slope.astype(BF)
+        act = act.astype(BF)
+        for a in range(2):
+            act_s[a ^ core, b ^ xy] = act[:, a * (step // 2) : (a + 1) * (step // 2)]
+    store(act_s.at[0], 0)
+    store(act_s.at[1], 1)
+    store(gp_s, 4)
+    for copy in stores:
+        copy.wait()
+
+
+def gather_dy_kernel(n, *refs):
+    blocks, (dy_ref, dyt_ref), dy_s = refs[:n], refs[n : n + 2], refs[n + 2]
+    _, _, z = here()
+    t, width = blocks[0].shape
+    for j in range(n):
+        at = pl.multiple_of(((z - j) & (n - 1)) * t, t)
+        dy_s[pl.ds(at, t), :] = blocks[j][...]
+    dy = dy_s[...]
+    dy_ref[...] = dy
+    dy_t = transposed(dy)
+    part = width // n
+    for b in range(n):
+        dyt_ref[b ^ z] = dy_t[b * part : (b + 1) * part]
+
+
+def d_up_kernel(dy_ref, gp_ref, wd_hbm, out_ref, wd_s, sem):
+    n = out_ref.shape[0]
+    step = wd_s.shape[1]
+    loads = [
+        pltpu.make_async_copy(wd_hbm.at[pl.ds(b * step, step)], wd_s.at[b], sem.at[b])
+        for b in range(n)
+    ]
+    for load in loads:
+        load.start()
+    _, _, z = here()
+    dy = dy_ref[...]
+    for b in range(n):
+        loads[b].wait()
+        d_act = nt(dy, wd_s[b])
+        slope = gp_ref[:, b * step : (b + 1) * step].astype(F32)
+        out_ref[b ^ z] = (slope * d_act).astype(BF)
+
+
+def scatter_blocks(outs, r, k, low, high):
+    keep_a, send_a, keep_b, send_b = outs
+    r_y, r_x = r >> 1, r & 1
+    (send_a if r_x else keep_a)[r_y, k] = low
+    (send_b if r_y else keep_b)[r_x, k] = high
+
+
+def grad_down_kernel(lo_ref, lr_ref, ro_ref, rr_ref, *outs):
+    n, part, tokens = lo_ref.shape
+    lo = lo_ref[...].reshape(n * part, tokens)
+    lr = lr_ref[...].reshape(n * part, tokens)
+    for r in range(4):
+        g = (mm(lo, ro_ref[r]) + mm(lr, rr_ref[r])).astype(BF)
+        for k in range(n):
+            low = g[k * part : k * part + part // 2]
+            scatter_blocks(outs, r, k, low, g[k * part + part // 2 : (k + 1) * part])
+
+
+def grad_up_kernel(lo_ref, lr_ref, ro_ref, rr_ref, *outs):
+    _, part, tokens = lo_ref.shape[1:]
+    lo = lo_ref[2].reshape(4 * part, tokens)
+    lr = lr_ref[2].reshape(4 * part, tokens)
+    for k in range(ro_ref.shape[0]):
+        g = (mm(lo, ro_ref[k]) + mm(lr, rr_ref[k])).astype(BF)
+        for r in range(4):
+            low = g[r * part : r * part + part // 2]
+            scatter_blocks(outs, r, k, low, g[r * part + part // 2 : (r + 1) * part])
+
+
+def grad_attn_kernel(lo_ref, lr_ref, ro_ref, rr_ref, *outs):
+    _, part, tokens = lo_ref.shape[1:]
+    left = [ref[i].reshape(4 * part, tokens) for i in range(2) for ref in (lo_ref, lr_ref)]
+    width = ro_ref.shape[2]
+    cut = (width * 3 // 4) // 256 * 256
+    rest = width * 3 // 4 - cut
+    for k in range(ro_ref.shape[0]):
+        tail = []
+        for ref in (ro_ref, rr_ref):
+            v = ref[k, :, cut:]
+            first = lax.broadcasted_iota(jnp.int32, v.shape, 1) < rest
+            tail.append((jnp.where(first, v, 0), jnp.where(first, 0, v)))
+        head = mm(left[0], ro_ref[k, :, :cut]) + mm(left[1], rr_ref[k, :, :cut])
+        mixed = (mm(left[0], tail[0][0]) + mm(left[1], tail[1][0])) + (
+            mm(left[2], tail[0][1]) + mm(left[3], tail[1][1])
+        )
+        g = jnp.concatenate([head, mixed], axis=1).astype(BF)
+        for r in range(4):
+            low = g[r * part : r * part + part // 2]
+            scatter_blocks(outs, r, k, low, g[r * part + part // 2 : (r + 1) * part])
+
+
+def first_sum_kernel(ka, ra, kb, rb, oa, ob):
+    oa[...] = (ka[1].astype(F32) + ra[1].astype(F32)).astype(BF)
+    ob[...] = (kb[1].astype(F32) + rb[1].astype(F32)).astype(BF)
+
+
+def second_sum_kernel(ka, ra, ra2, kb, rb, rb2, keep, send):
+    for i, (k_ref, r_ref, r2_ref) in enumerate(((ka, ra, ra2), (kb, rb, rb2))):
+        for k in range(4):
+            total = (k_ref[0, k].astype(F32) + r_ref[0, k].astype(F32)) + r2_ref[k].astype(F32)
+            (send if k & 1 else keep)[k >> 1, i] = total.astype(BF)
+
+
+def third_sum_kernel(keep, got, out):
+    out[...] = (keep[1].astype(F32) + got[1].astype(F32)).astype(BF)
+
+
+def total_of(keep, got, last, i):
+    return (keep[0, i].astype(F32) + got[0, i].astype(F32)) + last[i].astype(F32)
+
+
+def last_rows_kernel(keep, got, last, out):
+    half = keep.shape[2]
+    for i in range(2):
+        out[i * half : (i + 1) * half] = total_of(keep, got, last, i)
+
+
+def last_turned_kernel(keep, got, last, out):
+    out[...] = jnp.transpose(
+        jnp.concatenate([total_of(keep, got, last, i) for i in range(2)], axis=0)
+    )
+
+
+def last_split_kernel(keep, got, last, *outs):
+    half = keep.shape[2]
+    for i in range(2):
+        total = total_of(keep, got, last, i)
+        part = total.shape[1] // len(outs)
+        for j, out in enumerate(outs):
+            out[i * half : (i + 1) * half] = total[:, j * part : (j + 1) * part]
+
+
+def backward_kernel(
+    du_ref, dy_ref, mid_ref, gf_ref, q_ref, k_ref, v_ref, kc_ref, vc_ref, em_ref, len_ref,
+    wu_hbm, wo_hbm,
+    r_ref, dq_ref, dk_ref, dv_ref, dmid_ref, ggf_ref, gpe_ref,
+    wu_s, wo_s, dkc_s, dvc_s, dqt_s, sem,
+):
+    loads = [
+        pltpu.make_async_copy(wu_hbm, wu_s, sem.at[0]),
+        pltpu.make_async_copy(wo_hbm, wo_s, sem.at[1]),
+    ]
+    for load in loads:
+        load.start()
+    _, _, z = here()
+    n = du_ref.shape[0]
+    width = dy_ref.shape[1]
+    step = wu_s.shape[1] // n
+    mid = mid_ref[...]
+    n2, r2 = normed(mid)
+    loads[0].wait()
+    d_h2 = nt(du_ref[z], wu_s[:, :step])
+    for b in range(1, n):
+        d_h2 = d_h2 + nt(du_ref[b ^ z], wu_s[:, b * step : (b + 1) * step])
+    ggf_ref[...] = jnp.sum(d_h2 * n2, axis=0, keepdims=True)
+    d_mid = dy_ref[...].astype(F32) + norm_back(n2, r2, gf_ref[...], d_h2)
+    dmid_ref[...] = d_mid
+    d_attn = d_mid.astype(BF)
+    loads[1].wait()
+    d_att = nt(d_attn, wo_s[...]).astype(BF)
+    scale = HEAD ** (-0.5)
+    kc_t = transposed(kc_ref[...])
+    for p in range(width // 128):
+        lanes = slice(128 * p, 128 * p + 128)
+        q2, do2 = q_ref[:, lanes], d_att[:, lanes]
+        q_pair, do_pair = halves(q2), halves(do2)
+        kc_pair, vc_pair = halves(kc_ref[:, lanes]), halves(vc_ref[:, lanes])
+        dvc, dkc = 0.0, 0.0
+        for i in range(2):
+            probs = softmax_rows(nt(kc_pair[i], q2) * scale)
+            d_probs = nt(vc_pair[i], do2)
+            inner = jnp.sum(probs * d_probs, axis=0, keepdims=True)
+            d_scores = (probs * (d_probs - inner)).astype(BF)
+            dvc = dvc + mm(probs.astype(BF), do_pair[i])
+            dkc = dkc + mm(d_scores, q_pair[i])
+            first = 128 * p + HEAD * i
+            dqt_s[first : first + HEAD, :] = mm(kc_t[first : first + HEAD, :], d_scores)
+        dvc_s[:, lanes] = dvc.astype(BF)
+        dkc_s[:, lanes] = (dkc * scale).astype(BF)
+    em = em_ref[...]
+    dkc, dvc = dkc_s[...], dvc_s[...]
+    d_query = jnp.transpose(dqt_s[...] * scale)
+    d_key, d_value = mm(em, dkc), mm(em, dvc)
+    keep = lax.broadcasted_iota(jnp.int32, gpe_ref.shape, 0) < len_ref[z, 0]
+    gpe_ref[...] = jnp.where(keep, nt(k_ref[...], dkc) + nt(v_ref[...], dvc), 0.0)
+    part = width // n
+    for i, value in enumerate((d_query, d_key, d_value, d_mid)):
+        for b in range(n):
+            r_ref[b ^ z, :, i * part : (i + 1) * part] = value[:, b * part : (b + 1) * part].astype(BF)
+    dq_ref[...] = d_query.astype(BF)
+    dk_ref[...] = d_key.astype(BF)
+    dv_ref[...] = d_value.astype(BF)
+
+
+def output_kernel(
+    n, dq_ref, dk_ref, dv_ref, x_ref, ga_ref, dmid_ref, mid_ref, ao_ref, ar_ref,
+    wq_ref, wk_ref, wv_ref, wd_ref, *refs,
+):
+    outs, gga_ref, out_s, gi_s = refs[:n], refs[n], refs[n + 1], refs[n + 2]
+    core, xy, z = here()
+    d_h = nt(dq_ref[...], wq_ref[...]) + nt(dk_ref[...], wk_ref[...]) + nt(dv_ref[...], wv_ref[...])
+    n1, r1 = normed(x_ref[...].astype(F32))
+    gga_ref[...] = jnp.sum(d_h * n1, axis=0, keepdims=True)
+    gi_s[...] = (dmid_ref[...] + norm_back(n1, r1, ga_ref[...], d_h)).astype(BF)
+    total = mid_ref[...]
+    part = ao_ref.shape[2]
+    for r in range(4):
+        for a, ref in enumerate((ao_ref, ar_ref)):
+            first = pl.multiple_of(((r ^ xy) * 2 + (a ^ core)) * part, part)
+            total = total + mm(ref[r], wd_ref[pl.ds(first, part), :])
+    out_s[...] = total.astype(BF)
+    t = outs[0].shape[1]
+    for j in range(n):
+        at = pl.multiple_of(((z - j) & (n - 1)) * t, t)
+        outs[j][0] = out_s[pl.ds(at, t), :]
+        outs[j][1] = gi_s[pl.ds(at, t), :]
+
+
+def unpack_kernel(n, *refs):
+    _, _, z = here()
+    for j in range(n):
+        refs[n][(z + j) & (n - 1)] = refs[j][0]
+        refs[n + 1][(z + j) & (n - 1)] = refs[j][1]
+
+
+def fast(
+    inputs, w_query, w_key, w_value, w_out, w_up, w_down, gain_attn, gain_ffn, proj_e, lengths,
+    cotangent,
+):
+    n, t, width = inputs.shape
+    ff = w_up.shape[1]
+    k_block = proj_e.shape[1]
+    mine, k_dim = n * t, n * k_block
+    wide = width + mine
+    grid = Grid(lax.axis_size("rows"), n)
+    ga, gf = gain_attn[None], gain_ffn[None]
+
+    packed = call(
+        functools.partial(pack_kernel, n),
+        [sds(t, wide)] * n + [sds(t, width)] * n,
+        (inputs, proj_e, cotangent),
+    )
+    xe = [packed[0]] + [grid.send(packed[j], "z", j) for j in range(1, n)]
+    dyb = [packed[n]] + [grid.send(packed[n + j], "z", j) for j in range(1, n)]
+
+    square = (mine, width)
+    sixth = width // 8
+    out = [
+        sds(4, mine, ff // 8), sds(4, mine, ff // 8),
+        sds(3, 4, sixth, mine), sds(3, 4, sixth, mine),
+        sds(mine, ff), sds(*square), sds(*square), sds(*square),
+        sds(k_dim, width), sds(k_dim, width), sds(*square, dtype=F32), sds(*square),
+        sds(mine, k_dim),
+    ]
+    weights = (w_query, w_key, w_value, w_out, w_up)
+    scratch = [pltpu.VMEM(w.shape, BF) for w in weights] + [
+        pltpu.VMEM((2, 4, mine, ff // 8), BF),
+        pltpu.VMEM((2, 3, 4, sixth, mine), BF),
+    ]
+    scratch += [pltpu.VMEM(o.shape, o.dtype) for o in out[4:]]
+    scratch += [
+        pltpu.VMEM((k_dim, mine), BF),
+        pltpu.VMEM((width, mine), F32),
+        pltpu.SemaphoreType.DMA((len(weights),)),
+        pltpu.SemaphoreType.DMA((len(out),)),
+    ]
+    act_own, act_oth, lt_own, lt_oth, gp, q, k, v, kc, vc, mid, x_nat, em = call(
+        functools.partial(forward_kernel, n),
+        out,
+        (*xe, lengths, ga, gf, *weights),
+        [VM] * n + [SCALARS, VM, VM] + [MANY] * 5,
+        scratch,
+        [MANY] * len(out),
+        cost=4_000_000_000,
+    )
+    act_got = grid.send(act_oth, "c", 1)
+    dy, dyt = call(
+        functools.partial(gather_dy_kernel, n),
+        [sds(*square), sds(n, width // n, mine)],
+        dyb,
+        scratch=[pltpu.VMEM(square, BF)],
+    )
+    dyt_got = grid.send(dyt, "c", 1)
+    lt_got = grid.send(lt_oth, "c", 1)
+    du = call(
+        d_up_kernel,
+        [sds(n, mine, ff // n)],
+        (dy, gp, w_down),
+        [VM, VM, MANY],
+        [pltpu.VMEM((n, ff // n, width), BF), pltpu.SemaphoreType.DMA((n,))],
+        cost=1_300_000_000,
+    )[0]
+    du_got = grid.send(du, "c", 1)
+
+    def scatter(parts):
+        keep_a, send_a, keep_b, send_b = parts
+        got_a, got_b = grid.send(send_a, "x", 1), grid.send(send_b, "y", 1)
+        shape = keep_a.shape
+        next_a, next_b = call(
+            first_sum_kernel, [sds(*shape[1:])] * 2, (keep_a, got_a, keep_b, got_b)
+        )
+        got_a2, got_b2 = grid.send(next_a, "y", 1), grid.send(next_b, "x", 1)
+        keep, send = call(
+            second_sum_kernel,
+            [sds(2, 2, *shape[2:])] * 2,
+            (keep_a, got_a, got_a2, keep_b, got_b, got_b2),
+        )
+        got = lax.ppermute(send, "kc", [(i, i ^ 1) for i in range(n)])
+        third = call(third_sum_kernel, [sds(2, *shape[2:])], (keep, got))[0]
+        last = lax.ppermute(third, "kc", [(i, i ^ 2) for i in range(n)])
+        return keep, got, last
+
+    down_parts = [sds(2, n, width // n // 2, ff // 8)] * 4
+    g_down = scatter(
+        call(grad_down_kernel, down_parts, (dyt, dyt_got, act_own, act_got), cost=1_300_000_000)
+    )
+    up_parts = [sds(2, n, sixth // 2, ff // n)] * 4
+    g_up = scatter(
+        call(grad_up_kernel, up_parts, (lt_own, lt_got, du, du_got), cost=1_300_000_000)
+    )
+    r_own, dq, dk, dv, d_mid, ggf, gpe = call(
+        backward_kernel,
+        [
+            sds(n, mine, width), sds(*square), sds(*square), sds(*square),
+            sds(*square, dtype=F32), sds(1, width, dtype=F32), sds(mine, k_dim, dtype=F32),
+        ],
+        (du, dy, mid, gf, q, k, v, kc, vc, em, lengths, w_up, w_out),
+        [VM] * 10 + [SCALARS, MANY, MANY],
+        [
+            pltpu.VMEM(w_up.shape, BF), pltpu.VMEM(w_out.shape, BF),
+            pltpu.VMEM((k_dim, width), BF), pltpu.VMEM((k_dim, width), BF),
+            pltpu.VMEM((width, mine), F32), pltpu.SemaphoreType.DMA((2,)),
+        ],
+        cost=4_000_000_000,
+    )
+    r_got = grid.send(r_own, "c", 1)
+    attn_parts = [sds(2, n, sixth // 2, width)] * 4
+    g_attn = scatter(
+        call(grad_attn_kernel, attn_parts, (lt_own, lt_got, r_own, r_got), cost=1_600_000_000)
+    )
+    blocks = call(
+        functools.partial(output_kernel, n),
+        [sds(2, t, width)] * n + [sds(1, width, dtype=F32)],
+        (dq, dk, dv, x_nat, ga, d_mid, mid, act_own, act_oth, w_query, w_key, w_value, w_down),
+        scratch=[pltpu.VMEM(square, BF), pltpu.VMEM(square, BF)],
+        cost=2_500_000_000,
+    )
+    gga = blocks[n]
+    back = [blocks[0]] + [grid.send(blocks[j], "z", n - j) for j in range(1, n)]
+    output, grad_in = call(
+        functools.partial(unpack_kernel, n), [sds(*inputs.shape)] * 2, back
+    )
+    small = small_sum(grid, gpe, jnp.concatenate([gga, ggf], axis=0))
+    (g_up,) = call(last_rows_kernel, [sds(sixth, ff // n, dtype=F32)], g_up)
+    (g_down,) = call(last_turned_kernel, [sds(ff // 8, width // n, dtype=F32)], g_down)
+    attn = call(last_split_kernel, [sds(sixth, width // n, dtype=F32)] * 4, g_attn)
+    return (output, grad_in, *attn, g_up, g_down, *small)
+
+
+def small_sum(grid, d_e, gains):
+    n_rows, n_kc = grid.n_rows, grid.n_kc
+    e_rows, e_cols = d_e.shape[0] // n_rows, d_e.shape[1] // n_kc
     d_e = d_e.reshape(n_rows, e_rows, n_kc, e_cols).transpose(0, 2, 1, 3)
-    g_cols = width // n_rows
-    gains = jnp.stack([gg_attn, gg_ffn]).reshape(2, n_rows, g_cols).transpose(1, 0, 2)
+    g_cols = gains.shape[1] // n_rows
+    gains = gains.reshape(2, n_rows, g_cols).transpose(1, 0, 2)
     gains = jnp.broadcast_to(gains[:, None], (n_rows, n_kc, 2, g_cols))
     small = jnp.concatenate(
         [d_e.reshape(n_rows, n_kc, -1), gains.reshape(n_rows, n_kc, -1)], axis=2
     )
-    small = small.reshape(ny, nx, nc, n_kc, -1)
-    if nc > 1:
+    small = small.reshape(grid.ny, grid.nx, grid.nc, n_kc, -1)
+    if grid.nc > 1:
         small = grid.scatter_sum(small, 2, "c")
     small = grid.scatter_sum(small, 1, "x")
     small = grid.scatter_sum(small, 0, "y")
     small = grid.scatter_sum(small, 0, "z")
     n_e = e_rows * e_cols
     return (
-        output,
-        grad_in,
-        attn[0],
-        attn[1],
-        attn[2],
-        attn[3],
-        g_up,
-        g_down,
         small[n_e : n_e + g_cols],
         small[n_e + g_cols :],
         small[:n_e].reshape(e_rows, e_cols),
     )
+
+
+def local(*args):
+    inputs, w_up, proj_e = args[0], args[5], args[9]
+    n, t, width = inputs.shape
+    mine = n * t
+    fits = (
+        lax.axis_size("rows") == 8
+        and lax.axis_size("kc") == n == 4
+        and proj_e.shape == (mine, t)
+        and mine % 128 == 0
+        and width % 768 == 0
+        and w_up.shape[1] == 4 * width
+    )
+    return fast(*args) if fits else general(*args)
 
 
 def solution(mesh):

time: 371 us -> 205 us (0.55); the launches traced: 364 us -> 204 us
  matrix products: 73.6 us -> 0 us
  Pallas kernels: 0 us -> 58.3 us
  starting transfers between devices: 101 us -> 46.2 us
  local copies, waits for them, and re-layouts: 79.2 us -> 28.6 us
  other arithmetic: 24.3 us -> 0.91 us
  blocking collectives: 16.6 us -> 0 us
    dot_general x35 -> x0, matrix products: 70.7 us -> none  [the longest x14 32.3 us: t_mm(): return jnp.einsum('ta,tb->ab', left, right, preferred_element_type=F32)]
    pallas_call x0 -> x22, Pallas kernels: none -> 58.3 us  [call(): pl.pallas_call(body, out_shape=outs, in_specs=specs or [VM] * len(args),...]
    ppermute x39 -> x12, starting transfers between devices: 47.6 us -> 21.1 us  [send(): return lax.ppermute(value, 'kc', [(i, (i + shift) % n) for i in range(n)])]
    dynamic_slice x22 -> x0, local copies, waits for them, and re-layouts: 22.7 us -> none  [the longest x4 9.77 us: by_core(): other = lax.dynamic_index_in_dim(v, nc - 1 - grid.c, 2, keepdims=False)]
    another operation x9 -> x0, local copies, waits for them, and re-layouts: 18.3 us -> none
    all_gather x1 -> x0, blocking collectives: 16.6 us -> none  [local(): e_t = lax.all_gather(proj_e.T, 'kc', axis=0, tiled=True)]
    ppermute x37 -> x20, starting transfers between devices: 34.1 us -> 19.2 us  [send(): return lax.ppermute(value, 'rows', pairs)]
    ppermute x12 -> x6, starting transfers between devices: 19 us -> 5.87 us  [the longest x3 3.68 us: scatter(): last = lax.ppermute(third, 'kc', [(i, i ^ 2) for i in range(n)])]
  transfers between devices with their start and end apart: 88 -> 38, of which waited for: 41 -> 15; matrix products, arithmetic and copies ran while one was open for 39% -> 4% of each run, Pallas kernels for 0% -> 12%
where the time goes in v2:
time: 205 us; the launch traced here: 204 us
  waiting for transfers between devices  69.2 us (34%)
  Pallas kernels  58.3 us (28%)
  starting transfers between devices  46.2 us (23%)
  local copies, waits for them, and re-layouts  28.6 us (14%)
    pallas_call x22, Pallas kernels, call(): pl.pallas_call(body, out_shape=outs, in_specs=specs or [VM] * len(args),...  58.3 us
    ppermute x12, waiting for transfers between devices, send(): return lax.ppermute(value, 'kc', [(i, (i + shift) % n) for i in range(n)])  31.3 us
    ppermute x20, waiting for transfers between devices, send(): return lax.ppermute(value, 'rows', pairs)  26.5 us
    unnamed x97, local copies, waits for them, and re-layouts  23.5 us
    ppermute x12, starting transfers between devices, send(): return lax.ppermute(value, 'kc', [(i, (i + shift) % n) for i in range(n)])  21.1 us
    ppermute x20, starting transfers between devices, send(): return lax.ppermute(value, 'rows', pairs)  19.2 us
    ppermute x3, waiting for transfers between devices, scatter(): last = lax.ppermute(third, 'kc', [(i, i ^ 2) for i in range(n)])  11.4 us
  transfers between devices with their start and end apart: 38, of which 15 were waited for; matrix products, arithmetic and copies ran while one was open for 4% of the time, Pallas kernels for 12%

profile of v2, /device:TPU:0, one launch (start us, length us, event | category | flops | bytes accessed | tf_op | source)
XLA Modules:
  0.0 204.4 jit_solution(8526485975663686173)
XLA Ops:
  3.6 3.1 %collective-permute-start = (bf16[64,768]{1,0:T(8,128)(2,1)S(1)}, bf16[64,768]{1,0:T(8,128)(2,1)S(1)}, u32[]{:S(2)}, u32[]{:S(2)}) collective-permute-start(bf16[64,768]{1,0:T(8,128)(2,1)S(1)} %get-tuple-element.77), channel_id=1, source_target_pairs={{0,1},{1,2},{2,3},{3,0},{4,5},{5,6},{6,7},{7,4},{8,9},{9,10},{10,1... | collective-permute-start | bytes 294920 | tf_op jit(solution)/shard_map/ppermute | solution.py:57
  6.7 1.6 collective-permute-start.3
  8.3 1.1 collective-permute-start.4
  9.3 2.9 %collective-permute-start.5 = (bf16[64,1024]{1,0:T(8,128)(2,1)S(1)}, bf16[64,1024]{1,0:T(8,128)(2,1)S(1)}, u32[]{:S(2)}, u32[]{:S(2)}) collective-permute-start(bf16[64,1024]{1,0:T(8,128)(2,1)S(1)} %get-tuple-element.84), channel_id=1, source_target_pairs={{0,3},{1,0},{2,1},{3,2},{4,7},{5,4},{6,5},{7,6},{8,11},{9,8},{10,9... | collective-permute-start | bytes 393224 | tf_op jit(solution)/shard_map/ppermute | solution.py:57
  12.5 1.9 collective-permute-start.2
  16.5 10.6 %collective-permute-done.1.refs_2_ = bf16[64,768]{1,0:T(8,128)(2,1)S(1)} collective-permute-done((bf16[64,768]{1,0:T(8,128)(2,1)S(1)}, bf16[64,768]{1,0:T(8,128)(2,1)S(1)}, u32[]{:S(2)}, u32[]{:S(2)}) %collective-permute-start.1) | collective-permute-done | bytes 98336 | tf_op jit(solution)/shard_map/ppermute | solution.py:57
  28.2 14.7 %shard_map.205 = (bf16[4,256,384]{2,1,0:T(8,128)(2,1)S(1)}, bf16[4,256,384]{2,1,0:T(8,128)(2,1)S(1)}, bf16[3,4,96,256]{3,2,1,0:T(8,128)(2,1)S(1)}, bf16[3,4,96,2...) custom-call(bf16[64,1024]{1,0:T(8,128)(2,1)S(1)} %get-tuple-element., ...), custom_call_target="tpu_custom_call" | custom-call | flops 4000000000 | bytes 1000000 | tf_op jit(solution)/shard_map/pallas_call | solution.py:266
  44.6 1.4 copy-done.12
  46.0 5.0 %shard_map.206.du_ref.ro_ref = bf16[4,256,768]{2,1,0:T(8,128)(2,1)} custom-call(bf16[256,768]{1,0:T(8,128)(2,1)S(1)} %get-tuple-element.80.dy_ref, bf16[256,3072]{1,0:T(8,128)(2,1)S(1)} %copy-done.12, bf16[3072,768]{1,0:T(8,128)(2,1)} %wd_ref.1), custom_call_target="tpu_custom_call" | custom-call | flops 1300000000 | bytes 1000000 | tf_op jit(solution)/shard_map/pallas_call | solution.py:266
  51.0 12.3 %shard_map.207 = (bf16[4,256,768]{2,1,0:T(8,128)(2,1)}, bf16[256,768]{1,0:T(8,128)(2,1)S(1)}, bf16[256,768]{1,0:T(8,128)(2,1)S(1)}, bf16[256,768]{1,0:T(8,128)(2...) custom-call(bf16[4,256,768]{2,1,0:T(8,128)(2,1)} %shard_map.206.du_ref.ro_ref, ...), custom_call_target="tpu_custom_call" | custom-call | flops 4000000000 | bytes 1000000 | tf_op jit(solution)/shard_map/pallas_call | solution.py:266
  69.2 1.0 copy-done.21
  70.2 7.0 %shard_map.208 = (bf16[2,64,768]{2,1,0:T(8,128)(2,1)S(1)}, bf16[2,64,768]{2,1,0:T(8,128)(2,1)}, bf16[2,64,768]{2,1,0:T(8,128)(2,1)S(1)}, bf16[2,64,768]{2,1,0:T(8,128)(2,1)S(1)}, f32[1,768]{1,0:T(1,128)S(1)}) custom-call(bf16[256,768]{1,0:T(8,128)(2,1)S(1)} %copy-done.17, bf16[256,768]{1,0:T(8,128)(2,1)S(1)} %copy-done.19, bf16[256,768]{1,0:T(8,128)(2,1)S(1)} %copy-done.21, ...), custom_call_target="tpu_custom_call" | custom-call | flops 2500000000 | bytes 1000000 | tf_op jit(solution)/shard_map/pallas_call | solution.py:266
  79.4 1.2 reshape.48
  81.6 3.3 %shard_map.220 = (bf16[2,4,96,384]{3,2,1,0:T(8,128)(2,1)S(1)}, bf16[2,4,96,384]{3,2,1,0:T(8,128)(2,1)S(1)}, bf16[2,4,96,384]{3,2,1,0:T(8,128)(2,1)S(1)}, bf16[2,4,96,384]{3,2,1,0:T(8,128)(2,1)S(1)}) custom-call(bf16[4,192,256]{2,1,0:T(8,128)(2,1)S(1)} %copy-done.36, bf16[4,192,256]{2,1,0:T(8,128)(2,1)} %collective-permute-done.24.lr_ref, ...), custom_call_target="tpu_custom_call" | custom-call | flops 1300000000 | bytes 1000000 | tf_op jit(solution)/shard_map/pallas_call | solution.py:266
  85.0 1.6 collective-permute-start.26
  86.6 1.5 collective-permute-start.27
  88.1 3.4 %shard_map.210 = (bf16[2,4,48,768]{3,2,1,0:T(8,128)(2,1)S(1)}, bf16[2,4,48,768]{3,2,1,0:T(8,128)(2,1)S(1)}, bf16[2,4,48,768]{3,2,1,0:T(8,128)(2,1)S(1)}, bf16[2,4,48,768]{3,2,1,0:T(8,128)(2,1)S(1)}) custom-call(bf16[3,4,96,256]{3,2,1,0:T(8,128)(2,1)S(1)} %copy-done.42, bf16[3,4,96,256]{3,2,1,0:T(8,128)(2,1)} %collective-permute-done.9.lr_ref, ...), custom_call_target="tpu_custom_call" | custom-call | flops 1600000000 | bytes 1000000 | tf_op jit(solution)/shard_map/pallas_call | solution.py:266
  92.2 1.6 collective-permute-start.33
  93.8 7.5 %collective-permute-done.26.ra = bf16[2,4,96,384]{3,2,1,0:T(8,128)(2,1)S(1)} collective-permute-done((bf16[2,4,96,384]{3,2,1,0:T(8,128)(2,1)S(1)}, bf16[2,4,96,384]{3,2,1,0:T(8,128)(2,1)S(1)}, u32[]{:S(2)}, u32[]{:S(2)}) %collective-permute-start.26) | collective-permute-done | bytes 589856 | tf_op jit(solution)/shard_map/ppermute | solution.py:68
  102.5 1.5 collective-permute-start.28
  104.0 1.2 collective-permute-start.29
  105.7 3.5 %shard_map.215 = (bf16[2,4,48,768]{3,2,1,0:T(8,128)(2,1)S(1)}, bf16[2,4,48,768]{3,2,1,0:T(8,128)(2,1)S(1)}, bf16[2,4,48,768]{3,2,1,0:T(8,128)(2,1)S(1)}, bf16[2,4,48,768]{3,2,1,0:T(8,128)(2,1)S(1)}) custom-call(bf16[3,4,96,256]{3,2,1,0:T(8,128)(2,1)S(1)} %copy-done.42, bf16[3,4,96,256]{3,2,1,0:T(8,128)(2,1)} %collective-permute-done.9.lr_ref, ...), custom_call_target="tpu_custom_call" | custom-call | flops 1300000000 | bytes 1000000 | tf_op jit(solution)/shard_map/pallas_call | solution.py:266
  109.2 6.2 %collective-permute-done.33 = f32[2,4,2240]{2,1,0:T(4,128)S(1)} collective-permute-done((f32[2,4,2240]{2,1,0:T(4,128)S(1)}, f32[2,4,2240]{2,1,0:T(4,128)S(1)}, u32[]{:S(2)}, u32[]{:S(2)}) %collective-permute-start.33) | collective-permute-done | bytes 71712 | tf_op jit(solution)/shard_map/ppermute | solution.py:68
  115.5 1.5 collective-permute-start.18
  117.0 1.5 collective-permute-start.19
  118.5 6.6 %collective-permute-done.12.rb = bf16[2,4,48,768]{3,2,1,0:T(8,128)(2,1)S(1)} collective-permute-done((bf16[2,4,48,768]{3,2,1,0:T(8,128)(2,1)S(1)}, bf16[2,4,48,768]{3,2,1,0:T(8,128)(2,1)S(1)}, u32[]{:S(2)}, u32[]{:S(2)}) %collective-permute-start.12) | collective-permute-done | bytes 589856 | tf_op jit(solution)/shard_map/ppermute | solution.py:68
  125.1 3.6 %collective-permute-start.6 = (bf16[2,64,768]{2,1,0:T(8,128)(2,1)}, bf16[2,64,768]{2,1,0:T(8,128)(2,1)}, u32[]{:S(2)}, u32[]{:S(2)}) collective-permute-start(bf16[2,64,768]{2,1,0:T(8,128)(2,1)} %get-tuple-element.101), channel_id=1, source_target_pairs={{0,3},{1,0},{2,1},{3,2},{4,7},{5,4},{6,5},{7,6},{8,11},{9,8},{10,9... | collective-permute-start | bytes 589832 | tf_op jit(solution)/shard_map/ppermute | solution.py:57
  129.4 4.0 %collective-permute-done.18.ra = bf16[2,4,48,768]{3,2,1,0:T(8,128)(2,1)S(1)} collective-permute-done((bf16[2,4,48,768]{3,2,1,0:T(8,128)(2,1)S(1)}, bf16[2,4,48,768]{3,2,1,0:T(8,128)(2,1)S(1)}, u32[]{:S(2)}, u32[]{:S(2)}) %collective-permute-start.18) | collective-permute-done | bytes 589856 | tf_op jit(solution)/shard_map/ppermute | solution.py:68
  133.5 1.5 collective-permute-start.13
  138.1 1.1 collective-permute-start.20
  140.0 1.6 collective-permute-start.21
  142.2 1.2 collective-permute-done.13.ra2
  144.1 1.5 collective-permute-start.34
  145.6 1.1 copy-done.1
  150.2 1.6 collective-permute-start.7
  151.9 1.2 shard_map.212
  153.1 2.7 %collective-permute-start.8 = (bf16[2,64,768]{2,1,0:T(8,128)(2,1)S(1)}, bf16[2,64,768]{2,1,0:T(8,128)(2,1)S(1)}, u32[]{:S(2)}, u32[]{:S(2)}) collective-permute-start(bf16[2,64,768]{2,1,0:T(8,128)(2,1)S(1)} %copy-done.38), channel_id=1, source_target_pairs={{0,1},{1,2},{2,3},{3,0},{4,5},{5,6},{6,7},{7,4},{8,9},{9,10},{10,1... | collective-permute-start | bytes 589832 | tf_op jit(solution)/shard_map/ppermute | solution.py:57
  155.9 1.3 shard_map.217
  157.2 1.9 collective-permute-start.15
  161.1 1.0 collective-permute-start.35
  162.1 3.1 %collective-permute-done.8.refs_3_ = bf16[2,64,768]{2,1,0:T(8,128)(2,1)S(1)} collective-permute-done((bf16[2,64,768]{2,1,0:T(8,128)(2,1)S(1)}, bf16[2,64,768]{2,1,0:T(8,128)(2,1)S(1)}, u32[]{:S(2)}, u32[]{:S(2)}) %collective-permute-start.8) | collective-permute-done | bytes 196640 | tf_op jit(solution)/shard_map/ppermute | solution.py:57
  166.1 14.5 %collective-permute-done.35 = f32[2240]{0:T(1024)S(1)} collective-permute-done((f32[2240]{0:T(1024)S(1)}, f32[2240]{0:T(1024)S(1)}, u32[]{:S(2)}, u32[]{:S(2)}) %collective-permute-start.35) | collective-permute-done | bytes 8992 | tf_op jit(solution)/shard_map/ppermute | solution.py:57
  181.2 1.9 shard_map.209
  183.0 2.2 %collective-permute-done.36 = f32[2240]{0:T(1024)S(1)} collective-permute-done((f32[2240]{0:T(1024)S(1)}, f32[2240]{0:T(1024)S(1)}, u32[]{:S(2)}, u32[]{:S(2)}) %collective-permute-start.36) | collective-permute-done | bytes 8992 | tf_op jit(solution)/shard_map/ppermute | solution.py:57
  186.6 2.4 %collective-permute-start.16 = (bf16[2,48,768]{2,1,0:T(8,128)(2,1)S(1)}, bf16[2,48,768]{2,1,0:T(8,128)(2,1)S(1)}, u32[]{:S(2)}, u32[]{:S(2)}) collective-permute-start(bf16[2,48,768]{2,1,0:T(8,128)(2,1)S(1)} %shard_map.213), channel_id=1, source_target_pairs={{0,2},{1,3},{2,0},{3,1},{4,6},{5,7},{6,4},{7,5},{8,10},{9,11},{10,... | collective-permute-start | bytes 442376 | tf_op jit(solution)/shard_map/ppermute | solution.py:718
  190.3 4.2 %collective-permute-done.31.last = bf16[2,96,384]{2,1,0:T(8,128)(2,1)S(1)} collective-permute-done((bf16[2,96,384]{2,1,0:T(8,128)(2,1)S(1)}, bf16[2,96,384]{2,1,0:T(8,128)(2,1)S(1)}, u32[]{:S(2)}, u32[]{:S(2)}) %collective-permute-start.31) | collective-permute-done | bytes 147488 | tf_op jit(solution)/shard_map/ppermute | solution.py:718
  195.5 3.3 %collective-permute-done.16.last = bf16[2,48,768]{2,1,0:T(8,128)(2,1)S(1)} collective-permute-done((bf16[2,48,768]{2,1,0:T(8,128)(2,1)S(1)}, bf16[2,48,768]{2,1,0:T(8,128)(2,1)S(1)}, u32[]{:S(2)}, u32[]{:S(2)}) %collective-permute-start.16) | collective-permute-done | bytes 147488 | tf_op jit(solution)/shard_map/ppermute | solution.py:718
  199.7 3.9 %collective-permute-done.23.last = bf16[2,48,768]{2,1,0:T(8,128)(2,1)S(1)} collective-permute-done((bf16[2,48,768]{2,1,0:T(8,128)(2,1)S(1)}, bf16[2,48,768]{2,1,0:T(8,128)(2,1)S(1)}, u32[]{:S(2)}, u32[]{:S(2)}) %collective-permute-start.23) | collective-permute-done | bytes 147488 | tf_op jit(solution)/shard_map/ppermute | solution.py:718
  (168 shorter events, 37.8 us)
Async XLA Ops:
  3.6 8.9 %collective-permute-start = (bf16[64,768]{1,0:T(8,128)(2,1)S(1)}, bf16[64,768]{1,0:T(8,128)(2,1)S(1)}, u32[]{:S(2)}, u32[]{:S(2)}) collective-permute-start(bf16[64,768]{1,0:T(8,128)(2,1)S(1)} %get-tuple-element.77), channel_id=1, source_target_pairs={{0,1},{1,2},{2,3},{3,0},{4,5},{5,6},{6,7},{7,4},{8,9},{9,10},{10,1... | collective-permute-start | bytes 294920 | tf_op jit(solution)/shard_map/ppermute | solution.py:57
  6.7 20.7 %collective-permute-start.3 = (bf16[64,1024]{1,0:T(8,128)(2,1)S(1)}, bf16[64,1024]{1,0:T(8,128)(2,1)S(1)}, u32[]{:S(2)}, u32[]{:S(2)}) collective-permute-start(bf16[64,1024]{1,0:T(8,128)(2,1)S(1)} %get-tuple-element.82), channel_id=1, source_target_pairs={{0,1},{1,2},{2,3},{3,0},{4,5},{5,6},{6,7},{7,4},{8,9},{9,10},{10,1... | collective-permute-start | bytes 393224 | tf_op jit(solution)/shard_map/ppermute | solution.py:57
  8.3 19.1 %collective-permute-start.4 = (bf16[64,1024]{1,0:T(8,128)(2,1)S(1)}, bf16[64,1024]{1,0:T(8,128)(2,1)S(1)}, u32[]{:S(2)}, u32[]{:S(2)}) collective-permute-start(bf16[64,1024]{1,0:T(8,128)(2,1)S(1)} %get-tuple-element.83), channel_id=1, source_target_pairs={{0,2},{1,3},{2,0},{3,1},{4,6},{5,7},{6,4},{7,5},{8,10},{9,11},{10,... | collective-permute-start | bytes 393224 | tf_op jit(solution)/shard_map/ppermute | solution.py:57
  9.3 18.1 %collective-permute-start.5 = (bf16[64,1024]{1,0:T(8,128)(2,1)S(1)}, bf16[64,1024]{1,0:T(8,128)(2,1)S(1)}, u32[]{:S(2)}, u32[]{:S(2)}) collective-permute-start(bf16[64,1024]{1,0:T(8,128)(2,1)S(1)} %get-tuple-element.84), channel_id=1, source_target_pairs={{0,3},{1,0},{2,1},{3,2},{4,7},{5,4},{6,5},{7,6},{8,11},{9,8},{10,9... | collective-permute-start | bytes 393224 | tf_op jit(solution)/shard_map/ppermute | solution.py:57
  12.2 14.9 %collective-permute-start.1 = (bf16[64,768]{1,0:T(8,128)(2,1)S(1)}, bf16[64,768]{1,0:T(8,128)(2,1)S(1)}, u32[]{:S(2)}, u32[]{:S(2)}) collective-permute-start(bf16[64,768]{1,0:T(8,128)(2,1)S(1)} %get-tuple-element.78), channel_id=1, source_target_pairs={{0,2},{1,3},{2,0},{3,1},{4,6},{5,7},{6,4},{7,5},{8,10},{9,11},{10,... | collective-permute-start | bytes 294920 | tf_op jit(solution)/shard_map/ppermute | solution.py:57
  12.5 14.6 %collective-permute-start.2 = (bf16[64,768]{1,0:T(8,128)(2,1)S(1)}, bf16[64,768]{1,0:T(8,128)(2,1)S(1)}, u32[]{:S(2)}, u32[]{:S(2)}) collective-permute-start(bf16[64,768]{1,0:T(8,128)(2,1)S(1)} %get-tuple-element.79), channel_id=1, source_target_pairs={{0,3},{1,0},{2,1},{3,2},{4,7},{5,4},{6,5},{7,6},{8,11},{9,8},{10,9... | collective-permute-start | bytes 294920 | tf_op jit(solution)/shard_map/ppermute | solution.py:57
  65.5 22.6 %collective-permute-start.10 = (bf16[4,256,768]{2,1,0:T(8,128)(2,1)}, bf16[4,256,768]{2,1,0:T(8,128)(2,1)}, u32[]{:S(2)}, u32[]{:S(2)}) collective-permute-start(bf16[4,256,768]{2,1,0:T(8,128)(2,1)} %get-tuple-element.108.ro_ref), channel_id=1, source_target_pairs={{0,4},{4,0},{8,12},{12,8},{16,20},{20,16},{24,28},{28,24},{1,5},{5... | collective-permute-start | bytes 4718600 | tf_op jit(solution)/shard_map/ppermute | solution.py:68
  66.2 15.4 %collective-permute-start.25 = (bf16[4,256,384]{2,1,0:T(8,128)(2,1)S(1)}, bf16[4,256,384]{2,1,0:T(8,128)(2,1)}, u32[]{:S(2)}, u32[]{:S(2)}) collective-permute-start(bf16[4,256,384]{2,1,0:T(8,128)(2,1)S(1)} %get-tuple-element.99.ar_ref), channel_id=1, source_target_pairs={{0,4},{4,0},{8,12},{12,8},{16,20},{20,16},{24,28},{28,24},{1,5},{5... | collective-permute-start | bytes 2359304 | tf_op jit(solution)/shard_map/ppermute | solution.py:68
  66.2 14.8 %collective-permute-start.24 = (bf16[4,192,256]{2,1,0:T(8,128)(2,1)}, bf16[4,192,256]{2,1,0:T(8,128)(2,1)}, u32[]{:S(2)}, u32[]{:S(2)}) collective-permute-start(bf16[4,192,256]{2,1,0:T(8,128)(2,1)} %copy-done.35), channel_id=1, source_target_pairs={{0,4},{4,0},{8,12},{12,8},{16,20},{20,16},{24,28},{28,24},{1,5},{5... | collective-permute-start | bytes 1179656 | tf_op jit(solution)/shard_map/ppermute | solution.py:68
  66.7 38.5 %collective-permute-start.17 = (bf16[4,256,768]{2,1,0:T(8,128)(2,1)}, bf16[4,256,768]{2,1,0:T(8,128)(2,1)}, u32[]{:S(2)}, u32[]{:S(2)}) collective-permute-start(bf16[4,256,768]{2,1,0:T(8,128)(2,1)} %shard_map.206.du_ref.ro_ref), channel_id=1, source_target_pairs={{0,4},{4,0},{8,12},{12,8},{16,20},{20,16},{24,28},{28,24},{1,5},{5... | collective-permute-start | bytes 4718600 | tf_op jit(solution)/shard_map/ppermute | solution.py:68
  66.7 19.8 %collective-permute-start.9 = (bf16[3,4,96,256]{3,2,1,0:T(8,128)(2,1)}, bf16[3,4,96,256]{3,2,1,0:T(8,128)(2,1)}, u32[]{:S(2)}, u32[]{:S(2)}) collective-permute-start(bf16[3,4,96,256]{3,2,1,0:T(8,128)(2,1)} %copy-done.34), channel_id=1, source_target_pairs={{0,4},{4,0},{8,12},{12,8},{16,20},{20,16},{24,28},{28,24},{1,5},{5... | collective-permute-start | bytes 1769480 | tf_op jit(solution)/shard_map/ppermute | solution.py:68
  81.0 7.1 %copy-start.33 = (bf16[4,256,768]{2,1,0:T(8,128)(2,1)S(1)}, bf16[4,256,768]{2,1,0:T(8,128)(2,1)}, u32[]{:S(2)}) copy-start(bf16[4,256,768]{2,1,0:T(8,128)(2,1)} %get-tuple-element.108.ro_ref) | copy-start | bytes 4718596
  81.0 7.1 %copy-start.42 = (bf16[3,4,96,256]{3,2,1,0:T(8,128)(2,1)S(1)}, bf16[3,4,96,256]{3,2,1,0:T(8,128)(2,1)}, u32[]{:S(2)}) copy-start(bf16[3,4,96,256]{3,2,1,0:T(8,128)(2,1)} %copy-done.41) | copy-start | bytes 1769476
  81.0 11.1 %collective-permute-start.32 = (f32[2,2,4,2240]{3,2,1,0:T(4,128)S(1)}, f32[2,2,4,2240]{3,2,1,0:T(4,128)S(1)}, u32[]{:S(2)}, u32[]{:S(2)}) collective-permute-start(f32[2,2,4,2240]{3,2,1,0:T(4,128)S(1)} %fusion.1), channel_id=1, source_target_pairs={{0,4},{4,0},{8,12},{12,8},{16,20},{20,16},{24,28},{28,24},{1,5},{5... | collective-permute-start | bytes 430088 | tf_op jit(solution)/shard_map/ppermute | solution.py:68
  85.0 16.3 %collective-permute-start.26 = (bf16[2,4,96,384]{3,2,1,0:T(8,128)(2,1)S(1)}, bf16[2,4,96,384]{3,2,1,0:T(8,128)(2,1)S(1)}, u32[]{:S(2)}, u32[]{:S(2)}) collective-permute-start(bf16[2,4,96,384]{3,2,1,0:T(8,128)(2,1)S(1)} %get-tuple-element.131), channel_id=1, source_target_pairs={{0,8},{4,12},{8,0},{12,4},{16,24},{20,28},{24,16},{28,20},{1,9},{5... | collective-permute-start | bytes 1769480 | tf_op jit(solution)/shard_map/ppermute | solution.py:68
  86.6 14.9 %collective-permute-start.27 = (bf16[2,4,96,384]{3,2,1,0:T(8,128)(2,1)S(1)}, bf16[2,4,96,384]{3,2,1,0:T(8,128)(2,1)S(1)}, u32[]{:S(2)}, u32[]{:S(2)}) collective-permute-start(bf16[2,4,96,384]{3,2,1,0:T(8,128)(2,1)S(1)} %get-tuple-element.133), channel_id=1, source_target_pairs={{0,16},{4,20},{8,24},{12,28},{16,0},{20,4},{24,8},{28,12},{1,17},{... | collective-permute-start | bytes 1769480 | tf_op jit(solution)/shard_map/ppermute | solution.py:68
  91.5 25.4 %collective-permute-start.11 = (bf16[2,4,48,768]{3,2,1,0:T(8,128)(2,1)S(1)}, bf16[2,4,48,768]{3,2,1,0:T(8,128)(2,1)S(1)}, u32[]{:S(2)}, u32[]{:S(2)}) collective-permute-start(bf16[2,4,48,768]{3,2,1,0:T(8,128)(2,1)S(1)} %get-tuple-element.110), channel_id=1, source_target_pairs={{0,8},{4,12},{8,0},{12,4},{16,24},{20,28},{24,16},{28,20},{1,9},{5... | collective-permute-start | bytes 1769480 | tf_op jit(solution)/shard_map/ppermute | solution.py:68
  92.2 23.2 %collective-permute-start.33 = (f32[2,4,2240]{2,1,0:T(4,128)S(1)}, f32[2,4,2240]{2,1,0:T(4,128)S(1)}, u32[]{:S(2)}, u32[]{:S(2)}) collective-permute-start(f32[2,4,2240]{2,1,0:T(4,128)S(1)} %dynamic-slice_bitcast_fusion), channel_id=1, source_target_pairs={{0,8},{4,12},{8,0},{12,4},{16,24},{20,28},{24,16},{28,20},{1,9},{5... | collective-permute-start | bytes 215048 | tf_op jit(solution)/shard_map/ppermute | solution.py:68
  102.5 34.9 %collective-permute-start.28 = (bf16[4,96,384]{2,1,0:T(8,128)(2,1)S(1)}, bf16[4,96,384]{2,1,0:T(8,128)(2,1)S(1)}, u32[]{:S(2)}, u32[]{:S(2)}) collective-permute-start(bf16[4,96,384]{2,1,0:T(8,128)(2,1)S(1)} %get-tuple-element.134), channel_id=1, source_target_pairs={{0,16},{4,20},{8,24},{12,28},{16,0},{20,4},{24,8},{28,12},{1,17},{... | collective-permute-start | bytes 884744 | tf_op jit(solution)/shard_map/ppermute | solution.py:68
  104.0 35.3 %collective-permute-start.29 = (bf16[4,96,384]{2,1,0:T(8,128)(2,1)S(1)}, bf16[4,96,384]{2,1,0:T(8,128)(2,1)S(1)}, u32[]{:S(2)}, u32[]{:S(2)}) collective-permute-start(bf16[4,96,384]{2,1,0:T(8,128)(2,1)S(1)} %get-tuple-element.135), channel_id=1, source_target_pairs={{0,8},{4,12},{8,0},{12,4},{16,24},{20,28},{24,16},{28,20},{1,9},{5... | collective-permute-start | bytes 884744 | tf_op jit(solution)/shard_map/ppermute | solution.py:68
  105.2 19.8 %collective-permute-start.12 = (bf16[2,4,48,768]{3,2,1,0:T(8,128)(2,1)S(1)}, bf16[2,4,48,768]{3,2,1,0:T(8,128)(2,1)S(1)}, u32[]{:S(2)}, u32[]{:S(2)}) collective-permute-start(bf16[2,4,48,768]{3,2,1,0:T(8,128)(2,1)S(1)} %get-tuple-element.112), channel_id=1, source_target_pairs={{0,16},{4,20},{8,24},{12,28},{16,0},{20,4},{24,8},{28,12},{1,17},{... | collective-permute-start | bytes 1769480 | tf_op jit(solution)/shard_map/ppermute | solution.py:68
  109.2 28.2 %copy-start.2 = (bf16[2,4,48,768]{3,2,1,0:T(8,128)(2,1)}, bf16[2,4,48,768]{3,2,1,0:T(8,128)(2,1)S(1)}, u32[]{:S(2)}) copy-start(bf16[2,4,48,768]{3,2,1,0:T(8,128)(2,1)S(1)} %get-tuple-element.121.ka) | copy-start | bytes 1769476
  109.2 28.2 %copy-start.4 = (bf16[2,4,48,768]{3,2,1,0:T(8,128)(2,1)}, bf16[2,4,48,768]{3,2,1,0:T(8,128)(2,1)S(1)}, u32[]{:S(2)}) copy-start(bf16[2,4,48,768]{3,2,1,0:T(8,128)(2,1)S(1)} %get-tuple-element.123.kb) | copy-start | bytes 1769476
  115.5 18.0 %collective-permute-start.18 = (bf16[2,4,48,768]{3,2,1,0:T(8,128)(2,1)S(1)}, bf16[2,4,48,768]{3,2,1,0:T(8,128)(2,1)S(1)}, u32[]{:S(2)}, u32[]{:S(2)}) collective-permute-start(bf16[2,4,48,768]{3,2,1,0:T(8,128)(2,1)S(1)} %get-tuple-element.122), channel_id=1, source_target_pairs={{0,8},{4,12},{8,0},{12,4},{16,24},{20,28},{24,16},{28,20},{1,9},{5... | collective-permute-start | bytes 1769480 | tf_op jit(solution)/shard_map/ppermute | solution.py:68
  117.0 18.7 %collective-permute-start.19 = (bf16[2,4,48,768]{3,2,1,0:T(8,128)(2,1)S(1)}, bf16[2,4,48,768]{3,2,1,0:T(8,128)(2,1)S(1)}, u32[]{:S(2)}, u32[]{:S(2)}) collective-permute-start(bf16[2,4,48,768]{3,2,1,0:T(8,128)(2,1)S(1)} %get-tuple-element.124), channel_id=1, source_target_pairs={{0,16},{4,20},{8,24},{12,28},{16,0},{20,4},{24,8},{28,12},{1,17},{... | collective-permute-start | bytes 1769480 | tf_op jit(solution)/shard_map/ppermute | solution.py:68
  118.5 23.1 %copy-start.45 = (f32[2,4,2240]{2,1,0:T(4,128)}, f32[2,4,2240]{2,1,0:T(4,128)S(1)}, u32[]{:S(2)}) copy-start(f32[2,4,2240]{2,1,0:T(4,128)S(1)} %bitcast_add_fusion) | copy-start | bytes 215044
  125.1 12.3 %copy-start.8 = (bf16[2,4,48,768]{3,2,1,0:T(8,128)(2,1)}, bf16[2,4,48,768]{3,2,1,0:T(8,128)(2,1)S(1)}, u32[]{:S(2)}) copy-start(bf16[2,4,48,768]{3,2,1,0:T(8,128)(2,1)S(1)} %collective-permute-done.12.rb) | copy-start | bytes 1769476
  125.1 32.1 %collective-permute-start.6 = (bf16[2,64,768]{2,1,0:T(8,128)(2,1)}, bf16[2,64,768]{2,1,0:T(8,128)(2,1)}, u32[]{:S(2)}, u32[]{:S(2)}) collective-permute-start(bf16[2,64,768]{2,1,0:T(8,128)(2,1)} %get-tuple-element.101), channel_id=1, source_target_pairs={{0,3},{1,0},{2,1},{3,2},{4,7},{5,4},{6,5},{7,6},{8,11},{9,8},{10,9... | collective-permute-start | bytes 589832 | tf_op jit(solution)/shard_map/ppermute | solution.py:57
  133.5 9.9 %collective-permute-start.13 = (bf16[4,48,768]{2,1,0:T(8,128)(2,1)S(1)}, bf16[4,48,768]{2,1,0:T(8,128)(2,1)S(1)}, u32[]{:S(2)}, u32[]{:S(2)}) collective-permute-start(bf16[4,48,768]{2,1,0:T(8,128)(2,1)S(1)} %get-tuple-element.113), channel_id=1, source_target_pairs={{0,16},{4,20},{8,24},{12,28},{16,0},{20,4},{24,8},{28,12},{1,17},{... | collective-permute-start | bytes 884744 | tf_op jit(solution)/shard_map/ppermute | solution.py:68
  135.7 14.5 %collective-permute-start.14 = (bf16[4,48,768]{2,1,0:T(8,128)(2,1)}, bf16[4,48,768]{2,1,0:T(8,128)(2,1)}, u32[]{:S(2)}, u32[]{:S(2)}) collective-permute-start(bf16[4,48,768]{2,1,0:T(8,128)(2,1)} %get-tuple-element.114), channel_id=1, source_target_pairs={{0,8},{4,12},{8,0},{12,4},{16,24},{20,28},{24,16},{28,20},{1,9},{5... | collective-permute-start | bytes 884744 | tf_op jit(solution)/shard_map/ppermute | solution.py:68
  138.1 14.9 %collective-permute-start.20 = (bf16[4,48,768]{2,1,0:T(8,128)(2,1)}, bf16[4,48,768]{2,1,0:T(8,128)(2,1)}, u32[]{:S(2)}, u32[]{:S(2)}) collective-permute-start(bf16[4,48,768]{2,1,0:T(8,128)(2,1)} %get-tuple-element.125), channel_id=1, source_target_pairs={{0,16},{4,20},{8,24},{12,28},{16,0},{20,4},{24,8},{28,12},{1,17},{... | collective-permute-start | bytes 884744 | tf_op jit(solution)/shard_map/ppermute | solution.py:68
  140.0 15.8 %collective-permute-start.21 = (bf16[4,48,768]{2,1,0:T(8,128)(2,1)}, bf16[4,48,768]{2,1,0:T(8,128)(2,1)}, u32[]{:S(2)}, u32[]{:S(2)}) collective-permute-start(bf16[4,48,768]{2,1,0:T(8,128)(2,1)} %get-tuple-element.126), channel_id=1, source_target_pairs={{0,8},{4,12},{8,0},{12,4},{16,24},{20,28},{24,16},{28,20},{1,9},{5... | collective-permute-start | bytes 884744 | tf_op jit(solution)/shard_map/ppermute | solution.py:68
  144.1 15.0 %collective-permute-start.34 = (f32[4,2240]{1,0:T(4,128)}, f32[4,2240]{1,0:T(4,128)}, u32[]{:S(2)}, u32[]{:S(2)}) collective-permute-start(f32[4,2240]{1,0:T(4,128)} %dynamic-slice_bitcast_fusion.1), channel_id=1, source_target_pairs={{0,16},{4,20},{8,24},{12,28},{16,0},{20,4},{24,8},{28,12},{1,17},{... | collective-permute-start | bytes 107528 | tf_op jit(solution)/shard_map/ppermute | solution.py:68
  150.2 5.7 %copy-start.7 = (bf16[2,4,48,768]{3,2,1,0:T(8,128)(2,1)S(1)}, bf16[2,4,48,768]{3,2,1,0:T(8,128)(2,1)}, u32[]{:S(2)}) copy-start(bf16[2,4,48,768]{3,2,1,0:T(8,128)(2,1)} %copy-done.6) | copy-start | bytes 1769476
  150.2 10.9 %collective-permute-start.7 = (bf16[2,64,768]{2,1,0:T(8,128)(2,1)S(1)}, bf16[2,64,768]{2,1,0:T(8,128)(2,1)S(1)}, u32[]{:S(2)}, u32[]{:S(2)}) collective-permute-start(bf16[2,64,768]{2,1,0:T(8,128)(2,1)S(1)} %copy-done.40), channel_id=1, source_target_pairs={{0,2},{1,3},{2,0},{3,1},{4,6},{5,7},{6,4},{7,5},{8,10},{9,11},{10,... | collective-permute-start | bytes 589832 | tf_op jit(solution)/shard_map/ppermute | solution.py:57
  153.0 6.3 %copy-start.46 = (f32[2,4,2240]{2,1,0:T(4,128)S(1)}, f32[2,4,2240]{2,1,0:T(4,128)}, u32[]{:S(2)}) copy-start(f32[2,4,2240]{2,1,0:T(4,128)} %copy-done.45) | copy-start | bytes 215044
  153.1 12.2 %collective-permute-start.8 = (bf16[2,64,768]{2,1,0:T(8,128)(2,1)S(1)}, bf16[2,64,768]{2,1,0:T(8,128)(2,1)S(1)}, u32[]{:S(2)}, u32[]{:S(2)}) collective-permute-start(bf16[2,64,768]{2,1,0:T(8,128)(2,1)S(1)} %copy-done.38), channel_id=1, source_target_pairs={{0,1},{1,2},{2,3},{3,0},{4,5},{5,6},{6,7},{7,4},{8,9},{9,10},{10,1... | collective-permute-start | bytes 589832 | tf_op jit(solution)/shard_map/ppermute | solution.py:57
  155.7 25.4 %copy-start.32 = (bf16[2,64,768]{2,1,0:T(8,128)(2,1)S(1)}, bf16[2,64,768]{2,1,0:T(8,128)(2,1)}, u32[]{:S(2)}) copy-start(bf16[2,64,768]{2,1,0:T(8,128)(2,1)} %copy-done.31) | copy-start | bytes 589828
  155.7 30.2 %copy-start.14 = (bf16[2,2,96,384]{3,2,1,0:T(8,128)(2,1)S(1)}, bf16[2,2,96,384]{3,2,1,0:T(8,128)(2,1)}, u32[]{:S(2)}) copy-start(bf16[2,2,96,384]{3,2,1,0:T(8,128)(2,1)} %copy-done.13) | copy-start | bytes 884740
  155.7 30.1 %collective-permute-start.30 = (bf16[2,2,96,384]{3,2,1,0:T(8,128)(2,1)}, bf16[2,2,96,384]{3,2,1,0:T(8,128)(2,1)S(1)}, u32[]{:S(2)}, u32[]{:S(2)}) collective-permute-start(bf16[2,2,96,384]{3,2,1,0:T(8,128)(2,1)} %get-tuple-element.137), channel_id=1, source_target_pairs={{0,1},{1,0},{2,3},{3,2},{4,5},{5,4},{6,7},{7,6},{8,9},{9,8},{10,11... | collective-permute-start | bytes 884744 | tf_op jit(solution)/shard_map/ppermute | solution.py:716
  157.2 29.4 %collective-permute-start.15 = (bf16[2,2,48,768]{3,2,1,0:T(8,128)(2,1)S(1)}, bf16[2,2,48,768]{3,2,1,0:T(8,128)(2,1)S(1)}, u32[]{:S(2)}, u32[]{:S(2)}) collective-permute-start(bf16[2,2,48,768]{3,2,1,0:T(8,128)(2,1)S(1)} %get-tuple-element.116), channel_id=1, source_target_pairs={{0,1},{1,0},{2,3},{3,2},{4,5},{5,4},{6,7},{7,6},{8,9},{9,8},{10,11... | collective-permute-start | bytes 884744 | tf_op jit(solution)/shard_map/ppermute | solution.py:716
  159.1 29.9 %collective-permute-start.22 = (bf16[2,2,48,768]{3,2,1,0:T(8,128)(2,1)S(1)}, bf16[2,2,48,768]{3,2,1,0:T(8,128)(2,1)S(1)}, u32[]{:S(2)}, u32[]{:S(2)}) collective-permute-start(bf16[2,2,48,768]{3,2,1,0:T(8,128)(2,1)S(1)} %get-tuple-element.128), channel_id=1, source_target_pairs={{0,1},{1,0},{2,3},{3,2},{4,5},{5,4},{6,7},{7,6},{8,9},{9,8},{10,11... | collective-permute-start | bytes 884744 | tf_op jit(solution)/shard_map/ppermute | solution.py:716
  161.1 19.4 %collective-permute-start.35 = (f32[2240]{0:T(1024)S(1)}, f32[2240]{0:T(1024)S(1)}, u32[]{:S(2)}, u32[]{:S(2)}) collective-permute-start(f32[2240]{0:T(1024)S(1)} %get-tuple-element.163), channel_id=1, source_target_pairs={{0,1},{1,2},{2,3},{3,0},{4,5},{5,6},{6,7},{7,4},{8,9},{9,10},{10,1... | collective-permute-start | bytes 26888 | tf_op jit(solution)/shard_map/ppermute | solution.py:57
  165.3 17.8 %collective-permute-start.37 = (f32[2240]{0:T(1024)S(1)}, f32[2240]{0:T(1024)S(1)}, u32[]{:S(2)}, u32[]{:S(2)}) collective-permute-start(f32[2240]{0:T(1024)S(1)} %get-tuple-element.164), channel_id=1, source_target_pairs={{0,3},{1,0},{2,1},{3,2},{4,7},{5,4},{6,5},{7,6},{8,11},{9,8},{10,9... | collective-permute-start | bytes 26888 | tf_op jit(solution)/shard_map/ppermute | solution.py:57
  180.5 4.7 %collective-permute-start.36 = (f32[2240]{0:T(1024)S(1)}, f32[2240]{0:T(1024)S(1)}, u32[]{:S(2)}, u32[]{:S(2)}) collective-permute-start(f32[2240]{0:T(1024)S(1)} %get-tuple-element.165), channel_id=1, source_target_pairs={{0,2},{1,3},{2,0},{3,1},{4,6},{5,7},{6,4},{7,5},{8,10},{9,11},{10,... | collective-permute-start | bytes 26888 | tf_op jit(solution)/shard_map/ppermute | solution.py:57
  185.9 8.5 %collective-permute-start.31 = (bf16[2,96,384]{2,1,0:T(8,128)(2,1)S(1)}, bf16[2,96,384]{2,1,0:T(8,128)(2,1)S(1)}, u32[]{:S(2)}, u32[]{:S(2)}) collective-permute-start(bf16[2,96,384]{2,1,0:T(8,128)(2,1)S(1)} %shard_map.223), channel_id=1, source_target_pairs={{0,2},{1,3},{2,0},{3,1},{4,6},{5,7},{6,4},{7,5},{8,10},{9,11},{10,... | collective-permute-start | bytes 442376 | tf_op jit(solution)/shard_map/ppermute | solution.py:718
  186.6 12.2 %collective-permute-start.16 = (bf16[2,48,768]{2,1,0:T(8,128)(2,1)S(1)}, bf16[2,48,768]{2,1,0:T(8,128)(2,1)S(1)}, u32[]{:S(2)}, u32[]{:S(2)}) collective-permute-start(bf16[2,48,768]{2,1,0:T(8,128)(2,1)S(1)} %shard_map.213), channel_id=1, source_target_pairs={{0,2},{1,3},{2,0},{3,1},{4,6},{5,7},{6,4},{7,5},{8,10},{9,11},{10,... | collective-permute-start | bytes 442376 | tf_op jit(solution)/shard_map/ppermute | solution.py:718
  189.1 14.5 %collective-permute-start.23 = (bf16[2,48,768]{2,1,0:T(8,128)(2,1)S(1)}, bf16[2,48,768]{2,1,0:T(8,128)(2,1)S(1)}, u32[]{:S(2)}, u32[]{:S(2)}) collective-permute-start(bf16[2,48,768]{2,1,0:T(8,128)(2,1)S(1)} %shard_map.218), channel_id=1, source_target_pairs={{0,2},{1,3},{2,0},{3,1},{4,6},{5,7},{6,4},{7,5},{8,10},{9,11},{10,... | collective-permute-start | bytes 442376 | tf_op jit(solution)/shard_map/ppermute | solution.py:718
  (37 other events, 66.8 us)
